TPU v7x, 128 devices: a whole 4x4x4 slice. The times are simulated.
128 devices in a mesh: dp: 32 (over y, x, core), row: 2 (over z_hi), col: 2 (over z_lo).
Axes of the slice: x: 4, y: 4, z: 4 (z_hi: 2, z_lo: 2; z = z_hi * 2 + z_lo), core: 2. Of those that a mesh axis runs over, the one named last changes fastest.
Arguments:
- block_in: bfloat16 [16384, 768], P(('dp', 'row'), 'col'), may hold values from -6 to 6
- out_grad: float32 [16384, 768], P(('dp', 'row'), 'col'), may hold values from -6 to 6
- seq_lengths: int32 [32, 4], P('dp'), may hold values from 1 to 384, 512 in all within a row
- weight_qkv: float32 [768, 3, 2, 384], P('col', None, 'row', 'dp'), may hold values from -0.21875 to 0.21875
- first_qkv: float32 [768, 3, 2, 384], P('col', None, 'row', 'dp'), may hold values from -64 to 64
- second_qkv: float32 [768, 3, 2, 384], P('col', None, 'row', 'dp'), may hold values from 8.192 to 32.768
- weight_out: float32 [768, 2, 384], P('row', 'col', 'dp'), may hold values from -1.25 to 1.25
- first_out: float32 [768, 2, 384], P('row', 'col', 'dp'), may hold values from -16 to 16
- second_out: float32 [768, 2, 384], P('row', 'col', 'dp'), may hold values from 0.65536 to 2.62144
- weight_up: float32 [768, 2, 1536], P('col', 'row', 'dp'), may hold values from -0.21875 to 0.21875
- first_up: float32 [768, 2, 1536], P('col', 'row', 'dp'), may hold values from -24 to 24
- second_up: float32 [768, 2, 1536], P('col', 'row', 'dp'), may hold values from 1.47456 to 5.89824
- weight_down: float32 [3072, 2, 384], P('row', 'col', 'dp'), may hold values from -0.109375 to 0.109375
- first_down: float32 [3072, 2, 384], P('row', 'col', 'dp'), may hold values from -48 to 48
- second_down: float32 [3072, 2, 384], P('row', 'col', 'dp'), may hold values from 5.89824 to 23.59296
- col_params: float32 [6, 2, 384], P(None, 'col', 'dp'), as said below
- first_col: float32 [6, 2, 384], P(None, 'col', 'dp'), may hold values from -80 to 80
- second_col: float32 [6, 2, 384], P(None, 'col', 'dp'), may hold values from 16.384 to 65.536
- bias_qv: float32 [2, 2, 384], P(None, 'row', 'dp'), may hold values from -1.75 to 1.75
- first_qv: float32 [2, 2, 384], P(None, 'row', 'dp'), may hold values from -64 to 64
- second_qv: float32 [2, 2, 384], P(None, 'row', 'dp'), may hold values from 8.192 to 32.768
- bias_up: float32 [2, 1536], P('row', 'dp'), may hold values from -1.75 to 1.75
- first_bup: float32 [2, 1536], P('row', 'dp'), may hold values from -24 to 24
- second_bup: float32 [2, 1536], P('row', 'dp'), may hold values from 1.47456 to 5.89824
Outputs:
- block_out: float32 [16384, 768], P(('dp', 'row'), 'col')
- grad_in: float32 [16384, 768], P(('dp', 'row'), 'col')
- grad_qkv: float32 [768, 3, 2, 384], P('col', None, 'row', 'dp')
- moment_qkv: float32 [768, 3, 2, 384], P('col', None, 'row', 'dp')
- new_qkv: float32 [768, 3, 2, 384], P('col', None, 'row', 'dp')
- grad_outproj: float32 [768, 2, 384], P('row', 'col', 'dp')
- moment_outproj: float32 [768, 2, 384], P('row', 'col', 'dp')
- new_outproj: float32 [768, 2, 384], P('row', 'col', 'dp')
- grad_upproj: float32 [768, 2, 1536], P('col', 'row', 'dp')
- moment_upproj: float32 [768, 2, 1536], P('col', 'row', 'dp')
- new_upproj: float32 [768, 2, 1536], P('col', 'row', 'dp')
- grad_downproj: float32 [3072, 2, 384], P('row', 'col', 'dp')
- moment_downproj: float32 [3072, 2, 384], P('row', 'col', 'dp')
- new_downproj: float32 [3072, 2, 384], P('row', 'col', 'dp')
- grad_colvec: float32 [6, 2, 384], P(None, 'col', 'dp')
- moment_colvec: float32 [6, 2, 384], P(None, 'col', 'dp')
- new_colvec: float32 [6, 2, 384], P(None, 'col', 'dp')
- grad_qvbias: float32 [2, 2, 384], P(None, 'row', 'dp')
- moment_qvbias: float32 [2, 2, 384], P(None, 'row', 'dp')
- new_qvbias: float32 [2, 2, 384], P(None, 'row', 'dp')
- grad_upbias: float32 [2, 1536], P('row', 'dp')
- moment_upbias: float32 [2, 1536], P('row', 'dp')
- new_upbias: float32 [2, 1536], P('row', 'dp')
Inputs may be any that keep to these rules, and one draw needn't show every extreme that they name: `seq_lengths`: each row sums to 512; in every row the longest sequence has exactly 384 tokens. `col_params`: rows 0 and 2 (the gains) lie in 0.6 to 1.4, the other rows are normal with deviation 0.3.
All inputs are finite; a program needn't handle non-finite values.
Results may differ from a plain program's by a relative error of at most 0.012.
The roundings to bfloat16 on the way count: a program that leaves them out, or rounds other values in their place, can miss the bound.
Values may be sent and summed in bfloat16 or wider, within the bound.
No kernel may reach another device: no remote copies, remote signals or barrier semaphores. Data moves between devices by JAX's collectives and lax.ppermute only.
A program may use at most 128 MiB of HBM per device.

v0:
```python
import functools

import jax
import jax.numpy as jnp
import numpy as np
from jax import lax
from jax.experimental import pallas as pl
from jax.experimental.pallas import tpu as pltpu
from jax.sharding import Mesh
from jax.sharding import PartitionSpec as P

HD = 64
D = 768
HALF = 384
FF = 3072
TOK = 512
QW = 256
QB = 2
N_DP = 32
STEP = 10

norm_eps = 1e-05
beta_one = 0.9
beta_two = 0.999
adam_eps = 1e-08
decay_rate = 0.1
neg_large = -1e30
step_rates = (0.25, 0.4, 0.25, 0.25, 0.3, 0.3, 0.3)

DP = ("y", "x", "core")
ALL = ("y", "x", "core", "row", "col")
bf16 = jnp.bfloat16
f32 = jnp.float32
VMEM = pltpu.VMEM


def swap_matrix():
    places = np.arange(192).reshape(4, 4, 12).transpose(1, 0, 2).reshape(192)
    return jnp.asarray(np.eye(192, dtype=np.float32)[places], dtype=bf16)


def dot_nn(a, b):
    return lax.dot_general(a, b, (((1,), (0,)), ((), ())), preferred_element_type=f32)


def dot_nt(a, b):
    return lax.dot_general(a, b, (((1,), (1,)), ((), ())), preferred_element_type=f32)


def dot_tn(a, b):
    return lax.dot_general(a, b, (((0,), (0,)), ((), ())), preferred_element_type=f32)


def masters_kernel(qkv_ref, out_ref, up_ref, down_ref, shard_ref):
    shard_ref[0:48, :] = jnp.concatenate([qkv_ref[:, 0, :], out_ref[:, 0, :]], axis=0).astype(bf16)
    shard_ref[48:96, :] = up_ref[...].astype(bf16)
    shard_ref[96:144, :] = jnp.concatenate(
        [down_ref[:, 0, HALF * m : HALF * m + HALF] for m in range(4)], axis=0
    ).astype(bf16)


def pack_masters(qkv, out, up, down):
    whole = pl.BlockSpec(memory_space=VMEM)
    return pl.pallas_call(
        masters_kernel,
        in_specs=[whole] * 4,
        out_specs=whole,
        out_shape=jax.ShapeDtypeStruct((144, HALF), bf16),
        name="pack_masters",
    )(qkv, out, up, down)


def moments(values):
    mean = jnp.sum(values, axis=1, keepdims=True) * (1.0 / D)
    centered = values - mean
    spread = jnp.sum(centered * centered, axis=1, keepdims=True) * (1.0 / D)
    inverse = lax.rsqrt(spread + norm_eps)
    return centered * inverse, inverse


def norm_back(grad_norm, unit, inverse, gain):
    scaled = grad_norm * gain
    total = jnp.sum(scaled, axis=1, keepdims=True) * (1.0 / D)
    crossed = jnp.sum(scaled * unit, axis=1, keepdims=True) * (1.0 / D)
    return inverse * (scaled - total - unit * crossed)


def gelu_pair(x):
    c = 0.7978845608028654
    square = x * x
    t = jnp.tanh(c * (x + 0.044715 * (square * x)))
    half = 0.5 * (1.0 + t)
    value = x * half
    slope = half + (0.5 * x) * (1.0 - t * t) * (c + (3.0 * 0.044715 * c) * square)
    return value, slope


def layer_kernel(
    place_ref,
    lengths_ref,
    x_ref,
    n1_ref,
    gl_ref,
    og_ref,
    vec_ref,
    bqkv_ref,
    bup_ref,
    swap_ref,
    gathered_ref,
    result_ref,
    gin_ref,
    keep_out,
    send_out,
    load_sem,
    store_sem,
    stage_s,
    wqkv_s,
    wout_s,
    wup_s,
    wdown_s,
    gattn_s,
    gup_s,
    gdown_s,
    small_s,
    buf_s,
    bias_s,
    q_s,
    k_s,
    v_s,
    vt_s,
    kt_s,
    p_s,
    at_s,
    a_s,
    mid_s,
    n2_s,
    act_s,
    gh_s,
    gn2_s,
    gqt_s,
):
    row = place_ref[0]
    col = place_ref[1]
    row_tok = pl.ds(pl.multiple_of(row * 256, 256), 256)
    row_half = pl.ds(pl.multiple_of(row * HALF, 128), HALF)
    col_half = pl.ds(pl.multiple_of(col * HALF, 128), HALF)

    core = place_ref[2]
    swap = swap_ref[...]
    load_attn = [
        pltpu.make_async_copy(gathered_ref.at[:, s, 0:48, :], stage_s.at[s], load_sem.at[s])
        for s in range(4)
    ]
    load_up = [
        pltpu.make_async_copy(
            gathered_ref.at[:, s, 48:96, :],
            wup_s.at[32 * (s // 2) : 32 * (s // 2) + 32, :, HALF * (s % 2) : HALF * (s % 2) + HALF],
            load_sem.at[4 + s],
        )
        for s in range(4)
    ]
    load_down = [
        pltpu.make_async_copy(gathered_ref.at[:, s, 96:144, :], stage_s.at[s], load_sem.at[8 + s])
        for s in range(4)
    ]
    for copy in load_attn + load_up:
        copy.start()

    def unswapped(s, g):
        block = stage_s[s, 4 * g : 4 * g + 4].reshape(192, HALF)
        return dot_nn(swap, block).astype(bf16)

    e0 = lengths_ref[0, 0]
    e1 = e0 + lengths_ref[0, 1]
    e2 = e1 + lengths_ref[0, 2]
    key_place = lax.broadcasted_iota(jnp.int32, (TOK, 1), 0)
    query_place = lax.broadcasted_iota(jnp.int32, (1, TOK), 1)

    def segment(places):
        return (
            (places >= e0).astype(jnp.int32)
            + (places >= e1).astype(jnp.int32)
            + (places >= e2).astype(jnp.int32)
        )

    allowed = (segment(key_place) == segment(query_place)) & (key_place <= query_place)
    bias_s[...] = jnp.where(allowed, 0.0, neg_large)

    for s in range(4):
        load_attn[s].wait()
        outer = HALF * (s // 2)
        inner = HALF * (s % 2)
        for g in range(8):
            block = unswapped(s, g)
            for j in range(3):
                wqkv_s[j, outer + 48 * g : outer + 48 * g + 48, inner : inner + HALF] = block[
                    48 * j : 48 * j + 48
                ]
            wout_s[inner + 48 * g : inner + 48 * g + 48, outer : outer + HALF] = block[144:192]
        load_down[s].start()

    n1 = n1_ref[...]
    queries = (dot_nt(n1, wqkv_s[0]) + bqkv_ref[0:1, :]).astype(bf16)
    q_s[...] = queries * jnp.asarray(HD**-0.5, bf16)
    keys = dot_nt(n1, wqkv_s[1]).astype(bf16)
    k_s[...] = keys
    kt_s[...] = keys.T
    values = (dot_nt(n1, wqkv_s[2]) + bqkv_ref[2:3, :]).astype(bf16)
    v_s[...] = values
    vt_s[...] = values.T

    lane = lax.broadcasted_iota(jnp.int32, (1, 128), 1)

    for pair in range(6):
        lanes = slice(pair * 128, pair * 128 + 128)
        q_pair = q_s[:, lanes]
        k_pair = k_s[:, lanes]
        for hh in range(2):
            mine = (lane < HD) if hh == 0 else (lane >= HD)
            q_one = jnp.where(mine, q_pair, jnp.zeros_like(q_pair))
            rows = slice(pair * 128 + hh * HD, pair * 128 + hh * HD + HD)
            for j in range(QB):
                kn = QW * (j + 1)
                qs = slice(QW * j, QW * j + QW)
                scores = dot_nt(k_pair[:kn], q_one[qs]) + bias_s[:kn, qs]
                top = jnp.max(scores, axis=0, keepdims=True)
                weights = jnp.exp(scores - top)
                total = jnp.sum(weights, axis=0, keepdims=True)
                probs = (weights * (1.0 / total)).astype(bf16)
                p_s[2 * pair + hh, :kn, qs] = probs
                at_s[rows, qs] = dot_nn(vt_s[rows, :kn], probs)

    a_s[...] = at_s[...].T.astype(bf16)

    mid = x_ref[...].astype(f32) + dot_nt(a_s[...], wout_s[...]) + vec_ref[4:5, :]
    mid_s[...] = mid
    unit2, inverse2 = moments(mid)
    n2_s[...] = (unit2 * vec_ref[2:3, :] + vec_ref[3:4, :]).astype(bf16)

    for s in range(4):
        load_up[s].wait()
        load_down[s].wait()
        outer = HALF * (s % 2)
        inner = (FF // 2) * (s // 2)
        for g in range(8):
            block = unswapped(s, g)
            for m in range(4):
                wdown_s[
                    outer + 48 * g : outer + 48 * g + 48, inner + HALF * m : inner + HALF * m + HALF
                ] = block[48 * m : 48 * m + 48]
    for chunk in range(4):
        units = slice(D * chunk, D * chunk + D)
        up = wup_s[16 * chunk : 16 * chunk + 16].reshape(D, D)
        for tile in range(2):
            ts = slice(256 * tile, 256 * tile + 256)
            hidden = dot_nt(n2_s[ts, :], up) + bup_ref[:, units]
            value, slope = gelu_pair(hidden)
            act_s[ts, units] = value.astype(bf16)
            grad_act = dot_nn(gl_ref[ts, :], wdown_s[:, units])
            grad_hidden = (grad_act * slope).astype(bf16)
            gh_s[ts, units] = grad_hidden
    for tile in range(2):
        ts = slice(256 * tile, 256 * tile + 256)
        gn2_s[ts, :] = dot_nn(gh_s[ts, :], wup_s[...].reshape(FF, D))
    result_ref[...] = (
        mid_s[row_tok, col_half]
        + vec_ref[5:6, col_half]
        + dot_nt(act_s[row_tok, :], wdown_s[col_half, :])
    )
    row_units = pl.ds(pl.multiple_of(row * (FF // 2), 128), FF // 2)
    gup_s[...] = dot_tn(gh_s[:, row_units], n2_s[:, col_half]).astype(bf16)
    gdown_s[...] = dot_tn(gl_ref[:, col_half], act_s[:, row_units]).astype(bf16)
    sums = jnp.sum(gh_s[:, row_units].astype(f32), axis=0, keepdims=True)
    for part in range(4):
        small_s[8 + part : 9 + part, :] = sums[:, HALF * part : HALF * part + HALF]

    ga_s = gh_s.at[:, 0:D]
    gq_s = gh_s.at[:, D : 2 * D]
    gk_s = gh_s.at[:, 2 * D : 3 * D]
    gv_s = gh_s.at[:, 3 * D : 4 * D]
    gm_s = act_s.at[:, 0:D]
    gn2 = gn2_s[...]
    unit2, inverse2 = moments(mid_s[...])
    delta = norm_back(gn2, unit2, inverse2, vec_ref[2:3, :])
    grad_mid = delta + gl_ref[...].astype(f32)
    gm_s[...] = grad_mid.astype(bf16)
    mid_s[...] = delta


    sums_rows = jnp.concatenate(
        [
            jnp.sum(gn2 * unit2, axis=0, keepdims=True),
            jnp.sum(gn2, axis=0, keepdims=True),
            jnp.sum(grad_mid, axis=0, keepdims=True),
            jnp.sum(gl_ref[...].astype(f32), axis=0, keepdims=True),
        ],
        axis=0,
    )
    gn2_s[0:4, :] = sums_rows
    small_s[2:6, :] = gn2_s[0:4, col_half]
    ga_s[...] = dot_nn(gm_s[...], wout_s[...]).astype(bf16)
    gattn_s[3] = dot_tn(gm_s[:, col_half], a_s[:, row_half]).astype(bf16)

    for pair in range(6):
        lanes = slice(pair * 128, pair * 128 + 128)
        q_pair = q_s[:, lanes]
        v_pair = v_s[:, lanes]
        g_pair = ga_s[:, lanes]
        grad_keys = []
        grad_values = []
        for hh in range(2):
            mine = (lane < HD) if hh == 0 else (lane >= HD)
            g_one = jnp.where(mine, g_pair, jnp.zeros_like(g_pair))
            rows = slice(pair * 128 + hh * HD, pair * 128 + hh * HD + HD)
            gk_parts = []
            gv_parts = []
            for j in range(2):
                kn = 256 * (j + 1)
                qs = slice(256 * j, 256 * j + 256)
                probs_low = p_s[2 * pair + hh, :kn, qs]
                probs = probs_low.astype(f32)
                product = probs * dot_nt(v_pair[:kn], g_one[qs])
                inner = jnp.sum(product, axis=0, keepdims=True)
                grad_scores = (product - probs * inner).astype(bf16)
                gv_parts.append(dot_nn(probs_low, g_pair[qs]))
                gk_parts.append(dot_nn(grad_scores, q_pair[qs]))
                gqt_s[rows, qs] = dot_nn(kt_s[rows, :kn], grad_scores)
            grad_keys.append((gk_parts[0] + gk_parts[1][:256], gk_parts[1][256:]))
            grad_values.append((gv_parts[0] + gv_parts[1][:256], gv_parts[1][256:]))
        for piece in range(2):
            ts = slice(256 * piece, 256 * piece + 256)
            gk_s[ts, lanes] = jnp.where(
                lane < HD, grad_keys[0][piece], grad_keys[1][piece]
            ).astype(bf16)
            gv_s[ts, lanes] = jnp.where(
                lane < HD, grad_values[0][piece], grad_values[1][piece]
            ).astype(bf16)

    gq_s[...] = (gqt_s[...].T * HD**-0.5).astype(bf16)

    n1_half = n1_ref[:, col_half]
    for j, source in enumerate((gq_s, gk_s, gv_s)):
        gattn_s[j] = dot_tn(source[:, row_half], n1_half).astype(bf16)
    small_s[6:7, :] = jnp.sum(gq_s[:, row_half].astype(f32), axis=0, keepdims=True)
    small_s[7:8, :] = jnp.sum(gv_s[:, row_half].astype(f32), axis=0, keepdims=True)
    gn1 = (
        dot_nn(gq_s[...], wqkv_s[0])
        + dot_nn(gk_s[...], wqkv_s[1])
        + dot_nn(gv_s[...], wqkv_s[2])
    )
    unit1, inverse1 = moments(x_ref[...].astype(f32))
    mid_s[...] += norm_back(gn1, unit1, inverse1, vec_ref[0:1, :])
    gn2_s[0:2, :] = jnp.concatenate(
        [jnp.sum(gn1 * unit1, axis=0, keepdims=True), jnp.sum(gn1, axis=0, keepdims=True)], axis=0
    )
    small_s[0:2, :] = gn2_s[0:2, col_half]
    small_s[12:16, :] = jnp.zeros((4, HALF), f32)
    gin_ref[...] = mid_s[row_tok, col_half] + og_ref[...]

    small = small_s[...].astype(bf16)
    for g in range(8):
        rows = slice(48 * g, 48 * g + 48)
        attn = dot_nn(swap, gattn_s[:, rows, :].reshape(192, HALF)).astype(bf16)
        down = jnp.concatenate([gdown_s[rows, HALF * m : HALF * m + HALF] for m in range(4)], axis=0)
        down = dot_nn(swap, down).astype(bf16)
        for i in range(4):
            to = 4 * g + i
            slot = jnp.bitwise_xor(core, to % 2)
            part = slice(48 * i, 48 * i + 48)
            buf_s[slot, to // 2, 0:48, :] = attn[part]
            buf_s[slot, to // 2, 48:96, :] = gup_s[48 * to : 48 * to + 48, :]
            buf_s[slot, to // 2, 96:144, :] = down[part]
            buf_s[slot, to // 2, 144:160, :] = small
    store_send = pltpu.make_async_copy(buf_s.at[1], send_out, store_sem.at[0])
    store_keep = pltpu.make_async_copy(buf_s.at[0], keep_out, store_sem.at[1])
    store_send.start()
    store_keep.start()
    store_send.wait()
    store_keep.wait()


def layer(place, lengths, *operands):
    smem = pl.BlockSpec(memory_space=pltpu.SMEM)
    whole = pl.BlockSpec(memory_space=VMEM)
    anywhere = pl.BlockSpec(memory_space=pl.ANY)
    return pl.pallas_call(
        layer_kernel,
        in_specs=[smem, smem] + [whole] * (len(operands) - 1) + [anywhere],
        out_specs=[whole, whole, anywhere, anywhere],
        out_shape=[
            jax.ShapeDtypeStruct((256, HALF), f32),
            jax.ShapeDtypeStruct((256, HALF), f32),
            jax.ShapeDtypeStruct((16, 160, HALF), bf16),
            jax.ShapeDtypeStruct((16, 160, HALF), bf16),
        ],
        scratch_shapes=[
            pltpu.SemaphoreType.DMA((12,)),
            pltpu.SemaphoreType.DMA((2,)),
            VMEM((4, N_DP, 48, HALF), bf16),
            VMEM((3, D, D), bf16),
            VMEM((D, D), bf16),
            VMEM((64, 48, D), bf16),
            VMEM((D, FF), bf16),
            VMEM((4, HALF, HALF), bf16),
            VMEM((FF // 2, HALF), bf16),
            VMEM((HALF, FF // 2), bf16),
            VMEM((16, HALF), f32),
            VMEM((2, 16, 160, HALF), bf16),
            VMEM((TOK, TOK), f32),
            VMEM((TOK, D), bf16),
            VMEM((TOK, D), bf16),
            VMEM((TOK, D), bf16),
            VMEM((D, TOK), bf16),
            VMEM((D, TOK), bf16),
            VMEM((12, TOK, TOK), bf16),
            VMEM((D, TOK), f32),
            VMEM((TOK, D), bf16),
            VMEM((TOK, D), f32),
            VMEM((TOK, D), bf16),
            VMEM((TOK, FF), bf16),
            VMEM((TOK, FF), bf16),
            VMEM((TOK, D), f32),
            VMEM((D, TOK), f32),
        ],
        compiler_params=pltpu.CompilerParams(vmem_limit_bytes=60 * 1024 * 1024),
        name="layer",
    )(place, lengths, *operands)


def adam_kernel(data_ref, *refs):
    parts_ref = refs[0]
    masters, firsts, seconds = refs[1:8], refs[8:15], refs[15:22]
    grads, news, updates = refs[22:29], refs[29:36], refs[36:43]
    total = parts_ref[0].astype(f32)
    for i in range(1, 16):
        total = total + parts_ref[i].astype(f32)
    data = data_ref[0]
    small = pltpu.roll(total[144:152], HALF - data * 12, 1)
    wide = jnp.concatenate([total[152 + m : 153 + m] for m in range(4)], axis=1)
    wide = pltpu.roll(jnp.broadcast_to(wide, (8, FF // 2)), FF // 2 - data * 48, 1)
    gradients = (
        total[0:36].reshape(36, 1, HALF),
        total[36:48].reshape(12, 1, HALF),
        total[48:96],
        jnp.concatenate([total[96 + 12 * m : 108 + 12 * m] for m in range(4)], axis=1).reshape(
            12, 1, 4 * HALF
        ),
        small[0:6, 0:12].reshape(6, 1, 12),
        small[6:8, 0:12].reshape(2, 1, 12),
        wide[0:1, 0:48],
    )
    for i in range(7):
        second_new, updated = adam_update(
            masters[i][...], firsts[i][...], seconds[i][...], gradients[i], step_rates[i]
        )
        grads[i][...] = gradients[i]
        news[i][...] = second_new
        updates[i][...] = updated


def update_masters(data, parts, masters, firsts, seconds):
    whole = pl.BlockSpec(memory_space=VMEM)
    shapes = [jax.ShapeDtypeStruct(m.shape, f32) for m in masters]
    results = pl.pallas_call(
        adam_kernel,
        in_specs=[pl.BlockSpec(memory_space=pltpu.SMEM)] + [whole] * 22,
        out_specs=[whole] * 21,
        out_shape=shapes * 3,
        compiler_params=pltpu.CompilerParams(vmem_limit_bytes=32 * 1024 * 1024),
        name="update_masters",
    )(data, parts, *masters, *firsts, *seconds)
    return results[0:7], results[7:14], results[14:21]


def adam_update(master, first_old, second_old, gradient, step_rate):
    first_new = beta_one * first_old + (1.0 - beta_one) * gradient
    second_new = beta_two * second_old + (1.0 - beta_two) * gradient * gradient
    ratio = (
        first_new
        / (1.0 - beta_one**STEP)
        / (jnp.sqrt(second_new / (1.0 - beta_two**STEP)) + adam_eps)
    )
    return (second_new, master - step_rate * (ratio + decay_rate * master))


def on_device(
    block_in,
    out_grad,
    seq_lengths,
    weight_qkv,
    first_qkv,
    second_qkv,
    weight_out,
    first_out,
    second_out,
    weight_up,
    first_up,
    second_up,
    weight_down,
    first_down,
    second_down,
    col_params,
    first_col,
    second_col,
    bias_qv,
    first_qv,
    second_qv,
    bias_up,
    first_bup,
    second_bup,
):
    def flat(qkv, out, up, down, col, qv, bup):
        return (
            qkv.transpose(1, 3, 2, 0).reshape(36, 1, HALF),
            out.transpose(2, 1, 0),
            up.transpose(1, 2, 0).reshape(48, HALF),
            down.transpose(2, 1, 0),
            col,
            qv,
            bup,
        )

    def unflat(qkv, out, up, down, col, qv, bup):
        return (
            qkv.reshape(3, 12, 1, HALF).transpose(3, 0, 2, 1),
            out.transpose(2, 1, 0),
            up.reshape(1, 48, HALF).transpose(2, 0, 1),
            down.transpose(2, 1, 0),
            col,
            qv,
            bup,
        )

    masters = flat(weight_qkv, weight_out, weight_up, weight_down, col_params, bias_qv, bias_up)
    firsts = flat(first_qkv, first_out, first_up, first_down, first_col, first_qv, first_bup)
    seconds = flat(second_qkv, second_out, second_up, second_down, second_col, second_qv, second_bup)
    gathered = lax.all_gather(pack_masters(*masters[:4]), ALL, axis=0, tiled=False)
    gathered = gathered.reshape(N_DP, 4, 144, HALF)

    small = jnp.concatenate(
        [col_params.reshape(72), bias_qv.reshape(24), bias_up.reshape(48), jnp.zeros(240, f32)]
    ).astype(bf16)
    small = jnp.concatenate([small.reshape(1, HALF), jnp.zeros((15, HALF), bf16)], axis=0)
    four = lax.all_gather(
        jnp.concatenate([block_in, small], axis=0), ("row", "col"), axis=0, tiled=False
    )

    def whole_rows(four):
        return four.reshape(2, 2, 256, HALF).transpose(0, 2, 1, 3).reshape(TOK, D)

    rows_full = whole_rows(four[:, 0:256])
    smalls = lax.all_gather(four[:, 256, 0:144], DP, axis=0, tiled=False)
    smalls = smalls.reshape(N_DP, 2, 2, 144).astype(f32)
    vec = smalls[:, 0, :, 0:72].reshape(N_DP, 2, 6, 12).transpose(2, 1, 0, 3).reshape(6, D)
    vec = jnp.concatenate([vec, jnp.zeros((2, D), f32)], axis=0)
    bqv = smalls[:, :, 0, 72:96].reshape(N_DP, 2, 2, 12).transpose(2, 1, 0, 3).reshape(2, D)
    bqkv = jnp.stack([bqv[0], jnp.zeros_like(bqv[0]), bqv[1]])
    bup = smalls[:, :, 0, 96:144].transpose(1, 0, 2).reshape(1, FF)
    grad_full = whole_rows(
        lax.all_gather(out_grad.astype(bf16), ("row", "col"), axis=0, tiled=False)
    )
    unit_one, _ = moments(rows_full.astype(f32))
    normed_one = (unit_one * vec[0:1] + vec[1:2]).astype(bf16)

    place = jnp.stack([lax.axis_index("row"), lax.axis_index("col"), lax.axis_index("core")])
    result, grad_in, keep, send = layer(
        place.astype(jnp.int32),
        seq_lengths,
        rows_full,
        normed_one,
        grad_full,
        out_grad,
        vec,
        bqkv,
        bup,
        swap_matrix(),
        gathered,
    )

    other = lax.ppermute(send, "core", [(0, 1), (1, 0)])
    both = (keep.astype(f32) + other.astype(f32)).astype(bf16)
    parts = lax.all_to_all(both, ("y", "x"), 0, 0, tiled=True)
    data = lax.axis_index(DP).astype(jnp.int32).reshape(1)
    grads, news, updates = update_masters(data, parts, masters, firsts, seconds)
    outputs = [result, grad_in]
    for triple in zip(unflat(*grads), unflat(*news), unflat(*updates)):
        outputs += triple
    return tuple(outputs)


def solution(mesh):
    fine = Mesh(mesh.devices.reshape(4, 4, 2, 2, 2), ALL)
    qkv_spec = P("col", None, "row", DP)
    out_spec = P("row", "col", DP)
    up_spec = P("col", "row", DP)
    down_spec = P("row", "col", DP)
    col_spec = P(None, "col", DP)
    qv_spec = P(None, "row", DP)
    bup_spec = P("row", DP)
    rows_spec = P(DP + ("row",), "col")
    params = (qkv_spec, out_spec, up_spec, down_spec, col_spec, qv_spec, bup_spec)
    triples = tuple(spec for spec in params for _ in range(3))
    return jax.shard_map(
        on_device,
        mesh=fine,
        in_specs=(rows_spec, rows_spec, P(DP, None)) + triples,
        out_specs=(rows_spec, rows_spec) + triples,
        check_vma=False,
    )
```

profile of v0, /device:TPU:1, one launch (start us, length us, event | category | flops | bytes accessed | tf_op | source)
XLA Modules:
  0.0 191.9 jit_solution(15105478270247968092)
XLA Ops:
  7.2 1.7 pack_masters.1
  8.9 0.7 convert_reduce_fusion.3
  9.6 0.1 concatenate.22
  9.7 0.7 convert.16
  10.4 0.7 convert_reduce_fusion.2
  11.1 0.1 concatenate.21
  11.2 0.1 pad.9.clone
  11.2 1.0 maximum_maximum_fusion
  12.3 14.6 %all-gather = bf16[1088,384]{1,0:T(8,128)(2,1)S(1)} all-gather(bf16[272,384]{1,0:T(8,128)(2,1)S(1)} %maximum_maximum_fusion), channel_id=2, replica_groups=mesh['y'=4,'x'=4,'core'=2,'row'=2,'col'=2] {'row','col'}, dimensions={0}, use_global_device_ids=true | all-gather | bytes 1044480 | tf_op jit(solution)/shard_map/all_gather | solution.py:544
  26.9 0.1 slice.46
  27.0 26.8 %all-gather.1 = bf16[128,1,144]{2,1,0:T(2,128)(2,1)S(1)} all-gather(bf16[4,1,144]{2,1,0:T(2,128)(2,1)S(1)} %slice.47), channel_id=3, replica_groups=mesh['y'=4,'x'=4,'core'=2,'row'=2,'col'=2] {'y','x','core'}, dimensions={0}, use_global_device_ids=true | all-gather | bytes 38016 | tf_op jit(solution)/shard_map/all_gather | solution.py:552
  53.7 0.4 convert_reduce_fusion.1
  54.1 0.1 reshape.223
  54.2 0.1 slice.54
  54.3 0.1 slice.51
  54.5 13.8 %all-gather.2 = bf16[1024,384]{1,0:T(8,128)(2,1)S(1)} all-gather(bf16[256,384]{1,0:T(8,128)(2,1)S(1)} %convert_element_type.41), channel_id=4, replica_groups=mesh['y'=4,'x'=4,'core'=2,'row'=2,'col'=2] {'row','col'}, dimensions={0}, use_global_device_ids=true | all-gather | bytes 983040 | tf_op jit(solution)/shard_map/all_gather | solution.py:560
  68.3 0.8 copy.65
  69.1 1.0 copy.75
  70.1 0.8 copy.61
  70.9 0.2 convert_reduce_fusion
  71.1 0.1 copy.72
  71.3 0.4 fusion.1
  71.7 0.7 reshape.208.bup_ref
  72.4 0.1 copy.67
  72.4 0.1 copy.68
  72.5 0.1 slice.42
  72.7 0.1 copy.69
  72.8 0.1 slice.44
  72.9 0.1 copy.62
  73.0 0.1 copy.66
  73.1 0.1 copy.63
  73.2 0.1 mul.55
  73.3 0.1 copy.64
  73.4 0.1 add.35
  73.5 0.1 reshape.207
  73.7 0.6 concatenate.25.vec_ref
  74.3 0.1 pad.2.clone
  74.4 0.6 pad_add_fusion.place_ref
  74.9 0.7 pad_maximum_fusion.bqkv_ref
  75.6 1.3 add_convert_fusion.1.n1_ref
  76.9 15.4 %all-gather.6.cloned.1.call-done = bf16[18432,384]{1,0:T(8,128)(2,1)} async-done(((bf16[144,384]{1,0:T(8,128)(2,1)}), bf16[18432,384]{1,0:T(8,128)(2,1)}) %all-gather.6.cloned.1.call-update) | async-done | bytes 14155792 | tf_op jit(solution)/shard_map/all_gather | solution.py:537
  92.2 45.9 %layer.1 = (f32[256,384]{1,0:T(8,128)}, f32[256,384]{1,0:T(8,128)}, bf16[16,160,384]{2,1,0:T(8,128)(2,1)}, bf16[16,160,384]{2,1,0:T(8,128)(2,1)}) custom-call(s32[3]{0:T(128)} %pad_add_fusion.place_ref, s32[1,4]{1,0:T(1,128)} %lengths_ref.1, bf16[512,768]{1,0:T(8,128)(2,1)} %bitcast.112, bf16[512,768]{1,0:T(8,128)(2,1)} %add_convert_fusion.1.n1_ref, ...), custom_call_target="tpu_custom_call" | custom-call | tf_op jit(solution)/shard_map/layer/pallas_call | solution.py:386
  138.2 0.3 collective-permute-start
  138.5 3.9 %collective-permute-done = bf16[16,160,384]{2,1,0:T(8,128)(2,1)S(1)} collective-permute-done((bf16[16,160,384]{2,1,0:T(8,128)(2,1)}, bf16[16,160,384]{2,1,0:T(8,128)(2,1)S(1)}, u32[]{:S(2)}, u32[]{:S(2)}) %collective-permute-start) | collective-permute-done | bytes 1966112 | tf_op jit(solution)/shard_map/ppermute | solution.py:580
  142.4 3.3 %add_convert_fusion = bf16[16,160,384]{2,1,0:T(8,128)(2,1)} fusion(bf16[16,160,384]{2,1,0:T(8,128)(2,1)S(1)} %collective-permute-done, bf16[16,160,384]{2,1,0:T(8,128)(2,1)} %get-tuple-element.50), kind=kLoop, calls=%fused_computation | loop fusion | flops 3932160 | bytes 5898240 | tf_op jit(solution)/shard_map/convert_element_type | solution.py:581
  146.0 6.7 %all-to-all-start = ((bf16[16,160,384]{2,1,0:T(8,128)(2,1)}), bf16[16,160,384]{2,1,0:T(8,128)(2,1)S(1)}, u32[]{:S(2)}, u32[]{:S(2)}) async-start(bf16[16,160,384]{2,1,0:T(8,128)(2,1)} %add_convert_fusion), calls=%async_computation | async-start | bytes 3932160 | tf_op jit(solution)/shard_map/all_to_all | solution.py:582
  152.7 30.6 %all-to-all-done.refs_0_ = bf16[16,160,384]{2,1,0:T(8,128)(2,1)S(1)} async-done(((bf16[16,160,384]{2,1,0:T(8,128)(2,1)}), bf16[16,160,384]{2,1,0:T(8,128)(2,1)S(1)}, u32[]{:S(2)}, u32[]{:S(2)}) %all-to-all-start) | async-done | bytes 1966112 | tf_op jit(solution)/shard_map/all_to_all | solution.py:582
  183.5 1.5 update_masters.1
  (60 shorter events, 0.3 us)
Async XLA Ops:
  7.2 85.1 %all-gather.6.cloned.1.call-start = ((), (), s32[]{:S(2)}) async-start(), calls=%async_computation.1 | async-start | bytes 14266368 | tf_op jit(solution)/shard_map/all_gather | solution.py:537
  12.3 42.2 %copy-start.22 = (f32[256,384]{1,0:T(8,128)S(1)}, f32[256,384]{1,0:T(8,128)}, u32[]{:S(2)}) copy-start(f32[256,384]{1,0:T(8,128)} %og_ref.1) | copy-start | bytes 1179652
  71.3 5.6 %copy-start.21 = (bf16[64,8,2,384]{3,1,2,0:T(8,128)(2,1)}, bf16[64,8,2,384]{3,1,2,0:T(8,128)(2,1)S(1)}, u32[]{:S(2)}) copy-start(bf16[64,8,2,384]{3,1,2,0:T(8,128)(2,1)S(1)} %copy.72) | copy-start | bytes 2359300
  138.2 4.3 %collective-permute-start = (bf16[16,160,384]{2,1,0:T(8,128)(2,1)}, bf16[16,160,384]{2,1,0:T(8,128)(2,1)S(1)}, u32[]{:S(2)}, u32[]{:S(2)}) collective-permute-start(bf16[16,160,384]{2,1,0:T(8,128)(2,1)} %get-tuple-element.51), channel_id=1, source_target_pairs={{0,4},{4,0},{1,5},{5,1},{2,6},{6,2},{3,7},{7,3},{8,12},{12,8},{9,1... | collective-permute-start | bytes 5898248 | tf_op jit(solution)/shard_map/ppermute | solution.py:580
  145.8 37.5 %copy-start = (f32[384,1,48]{0,2,1:T(8,128)S(1)}, f32[384,1,48]{0,2,1:T(8,128)}, u32[]{:S(2)}) copy-start(f32[384,1,48]{0,2,1:T(8,128)} %param.34) | copy-start | bytes 221188
  145.8 37.5 %copy-start.1 = (f32[1536,1,12]{0,1,2:T(1,128)S(1)}, f32[1536,1,12]{0,1,2:T(1,128)}, u32[]{:S(2)}) copy-start(f32[1536,1,12]{0,1,2:T(1,128)} %param.37) | copy-start | bytes 221188
  145.8 37.5 %copy-start.2 = (f32[384,3,1,12]{0,2,3,1:T(1,128)S(1)}, f32[384,3,1,12]{0,2,3,1:T(1,128)}, u32[]{:S(2)}) copy-start(f32[384,3,1,12]{0,2,3,1:T(1,128)} %param.28) | copy-start | bytes 165892
  145.8 37.5 %copy-start.3 = (f32[384,1,48]{0,2,1:T(8,128)S(1)}, f32[384,1,48]{0,2,1:T(8,128)}, u32[]{:S(2)}) copy-start(f32[384,1,48]{0,2,1:T(8,128)} %param.35) | copy-start | bytes 221188
  145.8 37.5 %copy-start.4 = (f32[1536,1,12]{0,1,2:T(1,128)S(1)}, f32[1536,1,12]{0,1,2:T(1,128)}, u32[]{:S(2)}) copy-start(f32[1536,1,12]{0,1,2:T(1,128)} %param.38) | copy-start | bytes 221188
  145.8 37.5 %copy-start.5 = (f32[384,1,48]{0,2,1:T(8,128)S(1)}, f32[384,1,48]{0,2,1:T(8,128)}, u32[]{:S(2)}) copy-start(f32[384,1,48]{0,2,1:T(8,128)} %param.36) | copy-start | bytes 221188
  145.8 37.5 %copy-start.6 = (f32[1536,1,12]{0,1,2:T(1,128)S(1)}, f32[1536,1,12]{0,1,2:T(1,128)}, u32[]{:S(2)}) copy-start(f32[1536,1,12]{0,1,2:T(1,128)} %param.39) | copy-start | bytes 221188
  145.8 37.5 %copy-start.7 = (f32[384,1,12]{0,1,2:T(1,128)S(1)}, f32[384,1,12]{0,1,2:T(1,128)}, u32[]{:S(2)}) copy-start(f32[384,1,12]{0,1,2:T(1,128)} %param.31) | copy-start | bytes 55300
  145.8 37.5 %copy-start.8 = (f32[384,3,1,12]{0,2,3,1:T(1,128)S(1)}, f32[384,3,1,12]{0,2,3,1:T(1,128)}, u32[]{:S(2)}) copy-start(f32[384,3,1,12]{0,2,3,1:T(1,128)} %param.29) | copy-start | bytes 165892
  145.8 37.5 %copy-start.9 = (f32[384,3,1,12]{0,2,3,1:T(1,128)S(1)}, f32[384,3,1,12]{0,2,3,1:T(1,128)}, u32[]{:S(2)}) copy-start(f32[384,3,1,12]{0,2,3,1:T(1,128)} %param.30) | copy-start | bytes 165892
  145.8 37.5 %copy-start.10 = (f32[384,1,12]{0,1,2:T(1,128)S(1)}, f32[384,1,12]{0,1,2:T(1,128)}, u32[]{:S(2)}) copy-start(f32[384,1,12]{0,1,2:T(1,128)} %param.32) | copy-start | bytes 55300
  145.9 37.5 %copy-start.11 = (f32[384,1,12]{0,1,2:T(1,128)S(1)}, f32[384,1,12]{0,1,2:T(1,128)}, u32[]{:S(2)}) copy-start(f32[384,1,12]{0,1,2:T(1,128)} %param.33) | copy-start | bytes 55300
  145.9 37.5 %copy-start.12 = (f32[6,1,12]{2,1,0:T(1,128)S(1)}, f32[6,1,12]{2,1,0:T(1,128)}, u32[]{:S(2)}) copy-start(f32[6,1,12]{2,1,0:T(1,128)} %refs_5_.1) | copy-start | bytes 868
  145.9 37.5 %copy-start.13 = (f32[6,1,12]{2,1,0:T(1,128)S(1)}, f32[6,1,12]{2,1,0:T(1,128)}, u32[]{:S(2)}) copy-start(f32[6,1,12]{2,1,0:T(1,128)} %refs_12_.1) | copy-start | bytes 868
  145.9 37.5 %copy-start.14 = (f32[6,1,12]{2,1,0:T(1,128)S(1)}, f32[6,1,12]{2,1,0:T(1,128)}, u32[]{:S(2)}) copy-start(f32[6,1,12]{2,1,0:T(1,128)} %refs_19_.1) | copy-start | bytes 868
  145.9 37.5 %copy-start.15 = (f32[2,1,12]{2,1,0:T(1,128)S(1)}, f32[2,1,12]{2,1,0:T(1,128)}, u32[]{:S(2)}) copy-start(f32[2,1,12]{2,1,0:T(1,128)} %refs_6_.1) | copy-start | bytes 292
  145.9 37.5 %copy-start.16 = (f32[2,1,12]{2,1,0:T(1,128)S(1)}, f32[2,1,12]{2,1,0:T(1,128)}, u32[]{:S(2)}) copy-start(f32[2,1,12]{2,1,0:T(1,128)} %refs_13_.1) | copy-start | bytes 292
  145.9 37.5 %copy-start.17 = (f32[2,1,12]{2,1,0:T(1,128)S(1)}, f32[2,1,12]{2,1,0:T(1,128)}, u32[]{:S(2)}) copy-start(f32[2,1,12]{2,1,0:T(1,128)} %refs_20_.1) | copy-start | bytes 292
  145.9 37.5 %copy-start.18 = (f32[1,48]{1,0:T(1,128)S(1)}, f32[1,48]{1,0:T(1,128)}, u32[]{:S(2)}) copy-start(f32[1,48]{1,0:T(1,128)} %refs_7_.1) | copy-start | bytes 580
  146.0 37.5 %copy-start.19 = (f32[1,48]{1,0:T(1,128)S(1)}, f32[1,48]{1,0:T(1,128)}, u32[]{:S(2)}) copy-start(f32[1,48]{1,0:T(1,128)} %refs_14_.1) | copy-start | bytes 580
  146.0 37.5 %copy-start.20 = (f32[1,48]{1,0:T(1,128)S(1)}, f32[1,48]{1,0:T(1,128)}, u32[]{:S(2)}) copy-start(f32[1,48]{1,0:T(1,128)} %refs_21_.1) | copy-start | bytes 580
  146.0 37.3 %all-to-all-start = ((bf16[16,160,384]{2,1,0:T(8,128)(2,1)}), bf16[16,160,384]{2,1,0:T(8,128)(2,1)S(1)}, u32[]{:S(2)}, u32[]{:S(2)}) async-start(bf16[16,160,384]{2,1,0:T(8,128)(2,1)} %add_convert_fusion), calls=%async_computation | async-start | bytes 3932160 | tf_op jit(solution)/shard_map/all_to_all | solution.py:582
Sparse Core Ops, SparseCore 0:
  11.5 80.6 all-gather.5
where the time goes:
time: 195 us; the launch traced here: 192 us
  blocking collectives  55.1 us (28%)
  waiting for transfers between devices  49.9 us (26%)
  Pallas kernels  49 us (25%)
  between operations  14.7 us (8%)
  other arithmetic  9.89 us (5%)
  starting transfers between devices  7.03 us (4%)
  local copies, waits for them, and re-layouts  6.23 us (3%)
    pallas_call x1, Pallas kernels, layer(): pl.pallas_call(layer_kernel, in_specs=[smem, smem] + [whole] * (len(opera...  45.9 us
    all_to_all x1, waiting for transfers between devices, on_device(): parts = lax.all_to_all(both, ('y', 'x'), 0, 0, tiled=True)  30.6 us
    all_gather x1, blocking collectives, on_device(): smalls = lax.all_gather(four[:, 256, 0:144], DP, axis=0, tiled=False)  26.8 us
    all_gather x1, waiting for transfers between devices, on_device(): lax.all_gather(pack_masters(*masters[:4]), ALL, axis=0, tiled=False)  15.4 us
    all_gather x1, blocking collectives, on_device(): lax.all_gather(jnp.concatenate([block_in, small], axis=0), ('row', 'col')...  14.6 us
    all_gather x1, blocking collectives, on_device(): lax.all_gather(out_grad.astype(bf16), ('row', 'col'), axis=0, tiled=False)  13.8 us
    all_to_all x1, starting transfers between devices, on_device(): parts = lax.all_to_all(both, ('y', 'x'), 0, 0, tiled=True)  6.67 us
    ppermute x1, waiting for transfers between devices, on_device(): other = lax.ppermute(send, 'core', [(0, 1), (1, 0)])  3.94 us
  transfers between devices with their start and end apart: 3, of which 3 were waited for; matrix products, arithmetic and copies ran while one was open for 7% of the time, Pallas kernels for 0%

commit v1 on v0

--- a/solution.py
+++ b/solution.py
@@ -88,40 +88,42 @@
 def gelu_pair(x):
     c = 0.7978845608028654
     square = x * x
-    t = jnp.tanh(c * (x + 0.044715 * (square * x)))
-    half = 0.5 * (1.0 + t)
+    t = jnp.tanh(x * (c + (0.044715 * c) * square))
+    half = 0.5 + 0.5 * t
     value = x * half
-    slope = half + (0.5 * x) * (1.0 - t * t) * (c + (3.0 * 0.044715 * c) * square)
+    slope = half + value * (1.0 - t) * (c + (3.0 * 0.044715 * c) * square)
     return value, slope
 
 
 def layer_kernel(
     place_ref,
     lengths_ref,
-    x_ref,
+    x_hbm,
     n1_ref,
-    gl_ref,
-    og_ref,
+    gl_hbm,
+    og_hbm,
     vec_ref,
     bqkv_ref,
     bup_ref,
     swap_ref,
     gathered_ref,
     result_ref,
-    gin_ref,
+    part_ref,
+    small_s,
     keep_out,
     send_out,
+    gqkv_out,
+    wqkv_out,
     load_sem,
     store_sem,
+    x_ref,
+    gl_ref,
+    og_ref,
     stage_s,
     wqkv_s,
     wout_s,
     wup_s,
     wdown_s,
-    gattn_s,
-    gup_s,
-    gdown_s,
-    small_s,
     buf_s,
     bias_s,
     q_s,
@@ -131,6 +133,7 @@
     kt_s,
     p_s,
     at_s,
+    share_s,
     a_s,
     mid_s,
     n2_s,
@@ -163,7 +166,11 @@
         pltpu.make_async_copy(gathered_ref.at[:, s, 96:144, :], stage_s.at[s], load_sem.at[8 + s])
         for s in range(4)
     ]
-    for copy in load_attn + load_up:
+    load_rows = [
+        pltpu.make_async_copy(source, target, load_sem.at[12 + i])
+        for i, (source, target) in enumerate(((x_hbm, x_ref), (gl_hbm, gl_ref), (og_hbm, og_ref)))
+    ]
+    for copy in load_attn + load_rows:
         copy.start()
 
     def unswapped(s, g):
@@ -197,6 +204,7 @@
                     48 * j : 48 * j + 48
                 ]
             wout_s[inner + 48 * g : inner + 48 * g + 48, outer : outer + HALF] = block[144:192]
+        load_up[s].start()
         load_down[s].start()
 
     n1 = n1_ref[...]
@@ -206,6 +214,8 @@
     k_s[...] = keys
     kt_s[...] = keys.T
     values = (dot_nt(n1, wqkv_s[2]) + bqkv_ref[2:3, :]).astype(bf16)
+    store_wqkv = pltpu.make_async_copy(wqkv_s, wqkv_out, store_sem.at[2])
+    store_wqkv.start()
     v_s[...] = values
     vt_s[...] = values.T
 
@@ -225,13 +235,17 @@
                 scores = dot_nt(k_pair[:kn], q_one[qs]) + bias_s[:kn, qs]
                 top = jnp.max(scores, axis=0, keepdims=True)
                 weights = jnp.exp(scores - top)
-                total = jnp.sum(weights, axis=0, keepdims=True)
-                probs = (weights * (1.0 / total)).astype(bf16)
-                p_s[2 * pair + hh, :kn, qs] = probs
-                at_s[rows, qs] = dot_nn(vt_s[rows, :kn], probs)
-
-    a_s[...] = at_s[...].T.astype(bf16)
-
+                share = 1.0 / jnp.sum(weights, axis=0, keepdims=True)
+                weights = weights.astype(bf16)
+                p_s[2 * pair + hh, :kn, qs] = weights
+                share_s[2 * pair + hh : 2 * pair + hh + 1, qs] = share
+                at_s[rows, qs] = (dot_nn(vt_s[rows, :kn], weights) * share).astype(bf16)
+
+    a_s[...] = at_s[...].T
+    share_t = share_s[...].T
+
+    for copy in load_rows:
+        copy.wait()
     mid = x_ref[...].astype(f32) + dot_nt(a_s[...], wout_s[...]) + vec_ref[4:5, :]
     mid_s[...] = mid
     unit2, inverse2 = moments(mid)
@@ -268,8 +282,12 @@
         + dot_nt(act_s[row_tok, :], wdown_s[col_half, :])
     )
     row_units = pl.ds(pl.multiple_of(row * (FF // 2), 128), FF // 2)
-    gup_s[...] = dot_tn(gh_s[:, row_units], n2_s[:, col_half]).astype(bf16)
-    gdown_s[...] = dot_tn(gl_ref[:, col_half], act_s[:, row_units]).astype(bf16)
+    grad_up = dot_tn(gh_s[:, row_units], n2_s[:, col_half]).astype(bf16)
+    stage_s[0] = grad_up.reshape(N_DP, 48, HALF)
+    for m in range(4):
+        quarter = pl.ds(pl.multiple_of(row * (FF // 2) + HALF * m, 128), HALF)
+        grad_down = dot_tn(gl_ref[:, col_half], act_s[:, quarter]).astype(bf16)
+        stage_s[1, 8 * m : 8 * m + 8] = grad_down.reshape(8, 48, HALF)
     sums = jnp.sum(gh_s[:, row_units].astype(f32), axis=0, keepdims=True)
     for part in range(4):
         small_s[8 + part : 9 + part, :] = sums[:, HALF * part : HALF * part + HALF]
@@ -299,7 +317,11 @@
     gn2_s[0:4, :] = sums_rows
     small_s[2:6, :] = gn2_s[0:4, col_half]
     ga_s[...] = dot_nn(gm_s[...], wout_s[...]).astype(bf16)
-    gattn_s[3] = dot_tn(gm_s[:, col_half], a_s[:, row_half]).astype(bf16)
+
+    def put_attn(j, grad):
+        stage_s[2, 8 * j : 8 * j + 8] = grad.astype(bf16).reshape(8, 48, HALF)
+
+    put_attn(3, dot_tn(gm_s[:, col_half], a_s[:, row_half]))
 
     for pair in range(6):
         lanes = slice(pair * 128, pair * 128 + 128)
@@ -310,21 +332,24 @@
         grad_values = []
         for hh in range(2):
             mine = (lane < HD) if hh == 0 else (lane >= HD)
-            g_one = jnp.where(mine, g_pair, jnp.zeros_like(g_pair))
+            head = 2 * pair + hh
+            g_all = (g_pair.astype(f32) * share_t[:, head : head + 1]).astype(bf16)
+            g_one = jnp.where(mine, g_all, jnp.zeros_like(g_all))
             rows = slice(pair * 128 + hh * HD, pair * 128 + hh * HD + HD)
             gk_parts = []
             gv_parts = []
             for j in range(2):
                 kn = 256 * (j + 1)
                 qs = slice(256 * j, 256 * j + 256)
-                probs_low = p_s[2 * pair + hh, :kn, qs]
-                probs = probs_low.astype(f32)
-                product = probs * dot_nt(v_pair[:kn], g_one[qs])
-                inner = jnp.sum(product, axis=0, keepdims=True)
-                grad_scores = (product - probs * inner).astype(bf16)
-                gv_parts.append(dot_nn(probs_low, g_pair[qs]))
+                weights_low = p_s[head, :kn, qs]
+                weights = weights_low.astype(f32)
+                grad_probs = dot_nt(v_pair[:kn], g_one[qs])
+                inner = jnp.sum(weights * grad_probs, axis=0, keepdims=True)
+                inner = inner * share_s[head : head + 1, qs]
+                grad_scores = (weights * (grad_probs - inner)).astype(bf16)
+                gv_parts.append(dot_nn(weights_low, g_all[qs]))
                 gk_parts.append(dot_nn(grad_scores, q_pair[qs]))
-                gqt_s[rows, qs] = dot_nn(kt_s[rows, :kn], grad_scores)
+                gqt_s[rows, qs] = (dot_nn(kt_s[rows, :kn], grad_scores) * HD**-0.5).astype(bf16)
             grad_keys.append((gk_parts[0] + gk_parts[1][:256], gk_parts[1][256:]))
             grad_values.append((gv_parts[0] + gv_parts[1][:256], gv_parts[1][256:]))
         for piece in range(2):
@@ -336,47 +361,79 @@
                 lane < HD, grad_values[0][piece], grad_values[1][piece]
             ).astype(bf16)
 
-    gq_s[...] = (gqt_s[...].T * HD**-0.5).astype(bf16)
+    gq_s[...] = gqt_s[...].T
+    store_gqkv = pltpu.make_async_copy(gh_s.at[:, D : 4 * D], gqkv_out, store_sem.at[3])
+    store_gqkv.start()
 
     n1_half = n1_ref[:, col_half]
-    for j, source in enumerate((gq_s, gk_s, gv_s)):
-        gattn_s[j] = dot_tn(source[:, row_half], n1_half).astype(bf16)
+    row_rows = pl.ds(pl.multiple_of(row * HALF, HALF), HALF)
+    put_attn(0, dot_nn(gqt_s[row_rows, :], n1_half))
+    put_attn(1, dot_tn(gk_s[:, row_half], n1_half))
+    put_attn(2, dot_tn(gv_s[:, row_half], n1_half))
+    small_s[0:2, :] = jnp.zeros((2, HALF), f32)
     small_s[6:7, :] = jnp.sum(gq_s[:, row_half].astype(f32), axis=0, keepdims=True)
     small_s[7:8, :] = jnp.sum(gv_s[:, row_half].astype(f32), axis=0, keepdims=True)
-    gn1 = (
-        dot_nn(gq_s[...], wqkv_s[0])
-        + dot_nn(gk_s[...], wqkv_s[1])
-        + dot_nn(gv_s[...], wqkv_s[2])
-    )
-    unit1, inverse1 = moments(x_ref[...].astype(f32))
-    mid_s[...] += norm_back(gn1, unit1, inverse1, vec_ref[0:1, :])
-    gn2_s[0:2, :] = jnp.concatenate(
-        [jnp.sum(gn1 * unit1, axis=0, keepdims=True), jnp.sum(gn1, axis=0, keepdims=True)], axis=0
-    )
-    small_s[0:2, :] = gn2_s[0:2, col_half]
     small_s[12:16, :] = jnp.zeros((4, HALF), f32)
-    gin_ref[...] = mid_s[row_tok, col_half] + og_ref[...]
-
-    small = small_s[...].astype(bf16)
+    part_ref[...] = mid_s[row_tok, col_half] + og_ref[...]
+
     for g in range(8):
-        rows = slice(48 * g, 48 * g + 48)
-        attn = dot_nn(swap, gattn_s[:, rows, :].reshape(192, HALF)).astype(bf16)
-        down = jnp.concatenate([gdown_s[rows, HALF * m : HALF * m + HALF] for m in range(4)], axis=0)
+        down = jnp.concatenate([stage_s[1, 8 * m + g] for m in range(4)], axis=0)
         down = dot_nn(swap, down).astype(bf16)
+        attn = jnp.concatenate([stage_s[2, 8 * j + g] for j in range(4)], axis=0)
+        attn = dot_nn(swap, attn).astype(bf16)
         for i in range(4):
             to = 4 * g + i
             slot = jnp.bitwise_xor(core, to % 2)
             part = slice(48 * i, 48 * i + 48)
             buf_s[slot, to // 2, 0:48, :] = attn[part]
-            buf_s[slot, to // 2, 48:96, :] = gup_s[48 * to : 48 * to + 48, :]
+            buf_s[slot, to // 2, 48:96, :] = stage_s[0, to]
             buf_s[slot, to // 2, 96:144, :] = down[part]
-            buf_s[slot, to // 2, 144:160, :] = small
     store_send = pltpu.make_async_copy(buf_s.at[1], send_out, store_sem.at[0])
     store_keep = pltpu.make_async_copy(buf_s.at[0], keep_out, store_sem.at[1])
     store_send.start()
     store_keep.start()
     store_send.wait()
     store_keep.wait()
+    store_wqkv.wait()
+    store_gqkv.wait()
+
+
+def input_kernel(
+    place_ref, x_ref, vec_ref, gqkv_ref, wqkv_ref, part_ref, some_ref, gin_ref, small_ref, gn1_s, back_s
+):
+    row_tok = pl.ds(pl.multiple_of(place_ref[0] * 256, 256), 256)
+    col_half = pl.ds(pl.multiple_of(place_ref[1] * HALF, 128), HALF)
+    for tile in range(2):
+        ts = slice(256 * tile, 256 * tile + 256)
+        gn1_s[ts, :] = dot_nn(gqkv_ref[ts, :], wqkv_ref[...].reshape(3 * D, D))
+    gn1 = gn1_s[...]
+    unit1, inverse1 = moments(x_ref[...].astype(f32))
+    back_s[...] = norm_back(gn1, unit1, inverse1, vec_ref[0:1, :])
+    gin_ref[...] = back_s[row_tok, col_half] + part_ref[...]
+    back_s[0:2, :] = jnp.concatenate(
+        [jnp.sum(gn1 * unit1, axis=0, keepdims=True), jnp.sum(gn1, axis=0, keepdims=True)], axis=0
+    )
+    small_ref[...] = some_ref[...]
+    small_ref[0:2, :] = back_s[0:2, col_half]
+
+
+def input_gradient(place, *operands):
+    whole = pl.BlockSpec(memory_space=VMEM)
+    return pl.pallas_call(
+        input_kernel,
+        in_specs=[pl.BlockSpec(memory_space=pltpu.SMEM)] + [whole] * len(operands),
+        out_specs=[whole] * 2,
+        out_shape=[
+            jax.ShapeDtypeStruct((256, HALF), f32),
+            jax.ShapeDtypeStruct((16, HALF), f32),
+        ],
+        scratch_shapes=[VMEM((TOK, D), f32), VMEM((TOK, D), f32)],
+        compiler_params=pltpu.CompilerParams(vmem_limit_bytes=32 * 1024 * 1024),
+        cost_estimate=pl.CostEstimate(
+            flops=6 * TOK * D * D, bytes_accessed=8 * 1024 * 1024, transcendentals=0
+        ),
+        name="input_gradient",
+    )(place, *operands)
 
 
 def layer(place, lengths, *operands):
@@ -385,27 +442,31 @@
     anywhere = pl.BlockSpec(memory_space=pl.ANY)
     return pl.pallas_call(
         layer_kernel,
-        in_specs=[smem, smem] + [whole] * (len(operands) - 1) + [anywhere],
-        out_specs=[whole, whole, anywhere, anywhere],
+        in_specs=[smem, smem, anywhere, whole, anywhere, anywhere]
+        + [whole] * (len(operands) - 5)
+        + [anywhere],
+        out_specs=[whole, whole, whole, anywhere, anywhere, anywhere, anywhere],
         out_shape=[
             jax.ShapeDtypeStruct((256, HALF), f32),
             jax.ShapeDtypeStruct((256, HALF), f32),
-            jax.ShapeDtypeStruct((16, 160, HALF), bf16),
-            jax.ShapeDtypeStruct((16, 160, HALF), bf16),
+            jax.ShapeDtypeStruct((16, HALF), f32),
+            jax.ShapeDtypeStruct((16, 144, HALF), bf16),
+            jax.ShapeDtypeStruct((16, 144, HALF), bf16),
+            jax.ShapeDtypeStruct((TOK, 3 * D), bf16),
+            jax.ShapeDtypeStruct((3, D, D), bf16),
         ],
         scratch_shapes=[
-            pltpu.SemaphoreType.DMA((12,)),
-            pltpu.SemaphoreType.DMA((2,)),
+            pltpu.SemaphoreType.DMA((15,)),
+            pltpu.SemaphoreType.DMA((4,)),
+            VMEM((TOK, D), bf16),
+            VMEM((TOK, D), bf16),
+            VMEM((256, HALF), f32),
             VMEM((4, N_DP, 48, HALF), bf16),
             VMEM((3, D, D), bf16),
             VMEM((D, D), bf16),
             VMEM((64, 48, D), bf16),
             VMEM((D, FF), bf16),
-            VMEM((4, HALF, HALF), bf16),
-            VMEM((FF // 2, HALF), bf16),
-            VMEM((HALF, FF // 2), bf16),
-            VMEM((16, HALF), f32),
-            VMEM((2, 16, 160, HALF), bf16),
+            VMEM((2, 16, 144, HALF), bf16),
             VMEM((TOK, TOK), f32),
             VMEM((TOK, D), bf16),
             VMEM((TOK, D), bf16),
@@ -413,14 +474,15 @@
             VMEM((D, TOK), bf16),
             VMEM((D, TOK), bf16),
             VMEM((12, TOK, TOK), bf16),
-            VMEM((D, TOK), f32),
+            VMEM((D, TOK), bf16),
+            VMEM((16, TOK), f32),
             VMEM((TOK, D), bf16),
             VMEM((TOK, D), f32),
             VMEM((TOK, D), bf16),
             VMEM((TOK, FF), bf16),
             VMEM((TOK, FF), bf16),
             VMEM((TOK, D), f32),
-            VMEM((D, TOK), f32),
+            VMEM((D, TOK), bf16),
         ],
         compiler_params=pltpu.CompilerParams(vmem_limit_bytes=60 * 1024 * 1024),
         name="layer",
@@ -428,15 +490,16 @@
 
 
 def adam_kernel(data_ref, *refs):
-    parts_ref = refs[0]
-    masters, firsts, seconds = refs[1:8], refs[8:15], refs[15:22]
-    grads, news, updates = refs[22:29], refs[29:36], refs[36:43]
+    parts_ref, smalls_ref = refs[0:2]
+    masters, firsts, seconds = refs[2:9], refs[9:16], refs[16:23]
+    grads, news, updates = refs[23:30], refs[30:37], refs[37:44]
     total = parts_ref[0].astype(f32)
     for i in range(1, 16):
         total = total + parts_ref[i].astype(f32)
     data = data_ref[0]
-    small = pltpu.roll(total[144:152], HALF - data * 12, 1)
-    wide = jnp.concatenate([total[152 + m : 153 + m] for m in range(4)], axis=1)
+    lows = jnp.sum(smalls_ref[...], axis=0)
+    small = pltpu.roll(lows[0:8], HALF - data * 12, 1)
+    wide = jnp.concatenate([lows[8 + m : 9 + m] for m in range(4)], axis=1)
     wide = pltpu.roll(jnp.broadcast_to(wide, (8, FF // 2)), FF // 2 - data * 48, 1)
     gradients = (
         total[0:36].reshape(36, 1, HALF),
@@ -458,17 +521,17 @@
         updates[i][...] = updated
 
 
-def update_masters(data, parts, masters, firsts, seconds):
+def update_masters(data, parts, smalls, masters, firsts, seconds):
     whole = pl.BlockSpec(memory_space=VMEM)
     shapes = [jax.ShapeDtypeStruct(m.shape, f32) for m in masters]
     results = pl.pallas_call(
         adam_kernel,
-        in_specs=[pl.BlockSpec(memory_space=pltpu.SMEM)] + [whole] * 22,
+        in_specs=[pl.BlockSpec(memory_space=pltpu.SMEM)] + [whole] * 23,
         out_specs=[whole] * 21,
         out_shape=shapes * 3,
         compiler_params=pltpu.CompilerParams(vmem_limit_bytes=32 * 1024 * 1024),
         name="update_masters",
-    )(data, parts, *masters, *firsts, *seconds)
+    )(data, parts, smalls, *masters, *firsts, *seconds)
     return results[0:7], results[7:14], results[14:21]
 
 
@@ -563,8 +626,9 @@
     normed_one = (unit_one * vec[0:1] + vec[1:2]).astype(bf16)
 
     place = jnp.stack([lax.axis_index("row"), lax.axis_index("col"), lax.axis_index("core")])
-    result, grad_in, keep, send = layer(
-        place.astype(jnp.int32),
+    place = place.astype(jnp.int32)
+    result, part, some, keep, send, gqkv, wqkv = layer(
+        place,
         seq_lengths,
         rows_full,
         normed_one,
@@ -579,9 +643,12 @@
 
     other = lax.ppermute(send, "core", [(0, 1), (1, 0)])
     both = (keep.astype(f32) + other.astype(f32)).astype(bf16)
+    both, part = lax.optimization_barrier((both, part))
     parts = lax.all_to_all(both, ("y", "x"), 0, 0, tiled=True)
+    grad_in, small = input_gradient(place, rows_full, vec, gqkv, wqkv, part, some)
+    smalls = lax.all_gather(small, DP, axis=0, tiled=False)
     data = lax.axis_index(DP).astype(jnp.int32).reshape(1)
-    grads, news, updates = update_masters(data, parts, masters, firsts, seconds)
+    grads, news, updates = update_masters(data, parts, smalls, masters, firsts, seconds)
     outputs = [result, grad_in]
     for triple in zip(unflat(*grads), unflat(*news), unflat(*updates)):
         outputs += triple

time: 195 us -> 212 us (1.087)
  blocking collectives: 55.1 us -> 90.3 us
  waiting for transfers between devices: 49.9 us -> 18.9 us
  local copies, waits for them, and re-layouts: 6.23 us -> 18.9 us
    all_gather x0 -> x1, blocking collectives: none -> 35.2 us  [on_device(): smalls = lax.all_gather(small, DP, axis=0, tiled=False)]
    all_to_all x1, waiting for transfers between devices: 30.6 us -> 0.01 us  [on_device(): parts = lax.all_to_all(both, ('y', 'x'), 0, 0, tiled=True)]
    unnamed x50 -> x64, local copies, waits for them, and re-layouts: 1.26 us -> 14 us
    pallas_call x1 -> x2, Pallas kernels: 45.9 us -> 46.2 us  [the longest x1 42.3 us: layer(): pl.pallas_call(layer_kernel, in_specs=[smem, smem, anywhere, whole, anywh...]
  transfers between devices with their start and end apart: 3 -> 3, of which waited for: 3 -> 2; matrix products, arithmetic and copies ran while one was open for 7% -> 6% of each run, Pallas kernels for 0% -> 2%
where the time goes in v1:
time: 212 us; the launch traced here: 209 us
  blocking collectives  90.3 us (43%)
  Pallas kernels  49.2 us (23%)
  waiting for transfers between devices  18.9 us (9%)
  local copies, waits for them, and re-layouts  18.9 us (9%)
  between operations  14.6 us (7%)
  other arithmetic  9.85 us (5%)
  starting transfers between devices  7.01 us (3%)
    pallas_call x1, Pallas kernels, layer(): pl.pallas_call(layer_kernel, in_specs=[smem, smem, anywhere, whole, anywh...  42.3 us
    all_gather x1, blocking collectives, on_device(): smalls = lax.all_gather(small, DP, axis=0, tiled=False)  35.2 us
    all_gather x1, blocking collectives, on_device(): smalls = lax.all_gather(four[:, 256, 0:144], DP, axis=0, tiled=False)  26.8 us
    all_gather x1, waiting for transfers between devices, on_device(): lax.all_gather(pack_masters(*masters[:4]), ALL, axis=0, tiled=False)  15.2 us
    all_gather x1, blocking collectives, on_device(): lax.all_gather(jnp.concatenate([block_in, small], axis=0), ('row', 'col')...  14.6 us
    unnamed x64, local copies, waits for them, and re-layouts  14 us
    all_gather x1, blocking collectives, on_device(): lax.all_gather(out_grad.astype(bf16), ('row', 'col'), axis=0, tiled=False)  13.8 us
    all_to_all x1, starting transfers between devices, on_device(): parts = lax.all_to_all(both, ('y', 'x'), 0, 0, tiled=True)  6.65 us
  transfers between devices with their start and end apart: 3, of which 2 were waited for; matrix products, arithmetic and copies ran while one was open for 6% of the time, Pallas kernels for 2%

profile of v1, /device:TPU:1, one launch (start us, length us, event | category | flops | bytes accessed | tf_op | source)
XLA Modules:
  0.0 208.8 jit_solution(18337255755544925648)
XLA Ops:
  7.2 1.7 pack_masters.1
  8.9 0.7 convert_reduce_fusion.3
  9.7 0.7 convert.16
  10.4 0.7 convert_reduce_fusion.2
  11.2 1.0 maximum_maximum_fusion
  12.3 14.6 %all-gather = bf16[1088,384]{1,0:T(8,128)(2,1)S(1)} all-gather(bf16[272,384]{1,0:T(8,128)(2,1)S(1)} %maximum_maximum_fusion), channel_id=2, replica_groups=mesh['y'=4,'x'=4,'core'=2,'row'=2,'col'=2] {'row','col'}, dimensions={0}, use_global_device_ids=true | all-gather | bytes 1044480 | tf_op jit(solution)/shard_map/all_gather | solution.py:607
  27.0 26.8 %all-gather.1 = bf16[128,1,144]{2,1,0:T(2,128)(2,1)S(1)} all-gather(bf16[4,1,144]{2,1,0:T(2,128)(2,1)S(1)} %slice.47), channel_id=3, replica_groups=mesh['y'=4,'x'=4,'core'=2,'row'=2,'col'=2] {'y','x','core'}, dimensions={0}, use_global_device_ids=true | all-gather | bytes 38016 | tf_op jit(solution)/shard_map/all_gather | solution.py:615
  53.7 0.4 convert_reduce_fusion.1
  54.2 0.1 slice.54
  54.3 0.1 slice.51
  54.5 13.8 %all-gather.2 = bf16[1024,384]{1,0:T(8,128)(2,1)S(1)} all-gather(bf16[256,384]{1,0:T(8,128)(2,1)S(1)} %convert_element_type.41), channel_id=4, replica_groups=mesh['y'=4,'x'=4,'core'=2,'row'=2,'col'=2] {'row','col'}, dimensions={0}, use_global_device_ids=true | all-gather | bytes 983040 | tf_op jit(solution)/shard_map/all_gather | solution.py:623
  68.3 0.8 copy.64
  69.1 1.1 copy.74
  70.2 0.8 copy.60
  71.0 0.2 convert_reduce_fusion
  71.2 0.1 copy.71
  71.4 0.4 fusion.1
  71.8 0.7 reshape.208.bup_ref
  73.1 0.1 copy.65
  73.6 0.1 reshape.207
  73.8 0.6 concatenate.25.vec_ref
  74.5 0.6 pad_add_fusion.place_ref
  75.0 0.7 pad_maximum_fusion.bqkv_ref
  75.7 1.3 add_convert_fusion.1.n1_ref
  77.0 15.2 %all-gather.7.cloned.1.call-done = bf16[18432,384]{1,0:T(8,128)(2,1)} async-done(((bf16[144,384]{1,0:T(8,128)(2,1)}), bf16[18432,384]{1,0:T(8,128)(2,1)}) %all-gather.7.cloned.1.call-update) | async-done | bytes 14155792 | tf_op jit(solution)/shard_map/all_gather | solution.py:600
  92.2 42.3 %layer.1 = (f32[256,384]{1,0:T(8,128)}, f32[256,384]{1,0:T(8,128)}, f32[16,384]{1,0:T(8,128)}, bf16[16,144,384]{2,1,0:T(8,128)(2,1)}, bf16[16,144,384]{2,1,0:T(8...) custom-call(s32[3]{0:T(128)} %pad_add_fusion.place_ref, s32[1,4]{1,0:T(1,128)} %lengths_ref.1, ...), custom_call_target="tpu_custom_call" | custom-call | tf_op jit(solution)/shard_map/layer/pallas_call | solution.py:443
  134.5 0.3 collective-permute-start
  134.9 3.7 %collective-permute-done = bf16[16,144,384]{2,1,0:T(8,128)(2,1)S(1)} collective-permute-done((bf16[16,144,384]{2,1,0:T(8,128)(2,1)}, bf16[16,144,384]{2,1,0:T(8,128)(2,1)S(1)}, u32[]{:S(2)}, u32[]{:S(2)}) %collective-permute-start) | collective-permute-done | bytes 1769504 | tf_op jit(solution)/shard_map/ppermute | solution.py:644
  138.5 3.2 %add_convert_fusion = bf16[16,144,384]{2,1,0:T(8,128)(2,1)} fusion(bf16[16,144,384]{2,1,0:T(8,128)(2,1)S(1)} %collective-permute-done, bf16[16,144,384]{2,1,0:T(8,128)(2,1)} %get-tuple-element.58), kind=kLoop, calls=%fused_computation | loop fusion | flops 3538944 | bytes 5308416 | tf_op jit(solution)/shard_map/convert_element_type | solution.py:645
  141.7 6.6 %all-to-all-start = ((bf16[16,144,384]{2,1,0:T(8,128)(2,1)}), bf16[16,144,384]{2,1,0:T(8,128)(2,1)S(1)}, u32[]{:S(2)}, u32[]{:S(2)}) async-start(bf16[16,144,384]{2,1,0:T(8,128)(2,1)} %add_convert_fusion), calls=%async_computation | async-start | bytes 3538944 | tf_op jit(solution)/shard_map/all_to_all | solution.py:647
  148.4 2.0 copy-done.2
  150.4 1.7 copy-done.3
  152.1 0.7 copy-done.16
  152.8 0.7 copy-done.20
  153.6 3.9 %input_gradient.1 = (f32[256,384]{1,0:T(8,128)}, f32[16,384]{1,0:T(8,128)S(1)}) custom-call(s32[3]{0:T(128)S(1)} %copy-done.20, bf16[512,768]{1,0:T(8,128)(2,1)S(1)} %bitcast.94, f32[8,768]{1,0:T(8,128)S(1)} %copy-done.7, bf16[512,2304]{1,0:T(8,128)(2,1)S(1)} %copy-done.3, bf16[3,768,768]{2,1,0:T(8,128)(2,1)S(1)} %copy-done.2, f32[256,384]{1,0:T(8,128)S(1)} %copy-done.4, ...), custom_call_target="tpu_custom_call" | custom-call | flops 1811939328 | bytes 8388608 | tf_op jit(solution)/shard_map/input_gradient/pallas_call | solution.py:422
  157.5 35.2 %all-gather.4 = f32[512,384]{1,0:T(8,128)S(1)} all-gather(f32[16,384]{1,0:T(8,128)S(1)} %get-tuple-element.65), channel_id=6, replica_groups=mesh['y'=4,'x'=4,'core'=2,'row'=2,'col'=2] {'y','x','core'}, dimensions={0}, use_global_device_ids=true | all-gather | bytes 811008 | tf_op jit(solution)/shard_map/all_gather | solution.py:649
  192.8 0.8 copy-done.15
  193.6 0.7 copy-done.17
  194.3 0.7 copy-done.18
  195.0 0.7 copy-done.21
  195.7 0.7 copy-done.22
  196.4 0.7 copy-done.23
  197.1 0.7 copy-done.24
  197.7 0.7 copy-done.25
  198.4 0.7 copy-done.26
  199.1 0.7 copy-done.27
  199.7 0.7 copy-done.28
  200.4 1.4 update_masters.1
  (76 shorter events, 1.7 us)
Async XLA Ops:
  7.2 85.1 %all-gather.7.cloned.1.call-start = ((), (), s32[]{:S(2)}) async-start(), calls=%async_computation.1 | async-start | bytes 14266368 | tf_op jit(solution)/shard_map/all_gather | solution.py:600
  12.3 42.2 %copy-start.29 = (f32[256,384]{1,0:T(8,128)S(1)}, f32[256,384]{1,0:T(8,128)}, u32[]{:S(2)}) copy-start(f32[256,384]{1,0:T(8,128)} %og_hbm.1) | copy-start | bytes 1179652
  71.4 5.7 %copy-start = (bf16[64,8,2,384]{3,1,2,0:T(8,128)(2,1)}, bf16[64,8,2,384]{3,1,2,0:T(8,128)(2,1)S(1)}, u32[]{:S(2)}) copy-start(bf16[64,8,2,384]{3,1,2,0:T(8,128)(2,1)S(1)} %copy.71) | copy-start | bytes 2359300
  134.5 4.0 %collective-permute-start = (bf16[16,144,384]{2,1,0:T(8,128)(2,1)}, bf16[16,144,384]{2,1,0:T(8,128)(2,1)S(1)}, u32[]{:S(2)}, u32[]{:S(2)}) collective-permute-start(bf16[16,144,384]{2,1,0:T(8,128)(2,1)} %get-tuple-element.59), channel_id=1, source_target_pairs={{0,4},{4,0},{1,5},{5,1},{2,6},{6,2},{3,7},{7,3},{8,12},{12,8},{9,1... | collective-permute-start | bytes 5308424 | tf_op jit(solution)/shard_map/ppermute | solution.py:644
  141.7 6.7 %copy-start.1 = (bf16[64,8,2,384]{3,1,2,0:T(8,128)(2,1)S(1)}, bf16[64,8,2,384]{3,1,2,0:T(8,128)(2,1)}, u32[]{:S(2)}) copy-start(bf16[64,8,2,384]{3,1,2,0:T(8,128)(2,1)} %copy-done) | copy-start | bytes 2359300
  141.7 6.7 %copy-start.4 = (f32[256,384]{1,0:T(8,128)S(1)}, f32[256,384]{1,0:T(8,128)}, u32[]{:S(2)}) copy-start(f32[256,384]{1,0:T(8,128)} %get-tuple-element.61.part_ref) | copy-start | bytes 1179652
  141.7 6.7 %copy-start.7 = (f32[8,768]{1,0:T(8,128)S(1)}, f32[8,768]{1,0:T(8,128)}, u32[]{:S(2)}) copy-start(f32[8,768]{1,0:T(8,128)} %concatenate.25.vec_ref) | copy-start | bytes 73732
  141.7 50.9 %all-to-all-start = ((bf16[16,144,384]{2,1,0:T(8,128)(2,1)}), bf16[16,144,384]{2,1,0:T(8,128)(2,1)S(1)}, u32[]{:S(2)}, u32[]{:S(2)}) async-start(bf16[16,144,384]{2,1,0:T(8,128)(2,1)} %add_convert_fusion), calls=%async_computation | async-start | bytes 3538944 | tf_op jit(solution)/shard_map/all_to_all | solution.py:647
  148.4 2.0 copy-start.2
  150.4 1.7 copy-start.3
  152.1 0.7 copy-start.16
  152.8 0.7 copy-start.20
  153.5 39.2 %copy-start.5 = (f32[384,1,48]{0,2,1:T(8,128)S(1)}, f32[384,1,48]{0,2,1:T(8,128)}, u32[]{:S(2)}) copy-start(f32[384,1,48]{0,2,1:T(8,128)} %param.34) | copy-start | bytes 221188
  153.5 39.2 %copy-start.6 = (f32[1536,1,12]{0,1,2:T(1,128)S(1)}, f32[1536,1,12]{0,1,2:T(1,128)}, u32[]{:S(2)}) copy-start(f32[1536,1,12]{0,1,2:T(1,128)} %param.37) | copy-start | bytes 221188
  153.5 39.2 %copy-start.8 = (f32[384,3,1,12]{0,2,3,1:T(1,128)S(1)}, f32[384,3,1,12]{0,2,3,1:T(1,128)}, u32[]{:S(2)}) copy-start(f32[384,3,1,12]{0,2,3,1:T(1,128)} %param.28) | copy-start | bytes 165892
  153.5 39.2 %copy-start.9 = (f32[384,1,48]{0,2,1:T(8,128)S(1)}, f32[384,1,48]{0,2,1:T(8,128)}, u32[]{:S(2)}) copy-start(f32[384,1,48]{0,2,1:T(8,128)} %param.35) | copy-start | bytes 221188
  153.5 39.2 %copy-start.10 = (f32[1536,1,12]{0,1,2:T(1,128)S(1)}, f32[1536,1,12]{0,1,2:T(1,128)}, u32[]{:S(2)}) copy-start(f32[1536,1,12]{0,1,2:T(1,128)} %param.38) | copy-start | bytes 221188
  153.5 39.2 %copy-start.11 = (f32[384,1,48]{0,2,1:T(8,128)S(1)}, f32[384,1,48]{0,2,1:T(8,128)}, u32[]{:S(2)}) copy-start(f32[384,1,48]{0,2,1:T(8,128)} %param.36) | copy-start | bytes 221188
  153.5 39.2 %copy-start.12 = (f32[1536,1,12]{0,1,2:T(1,128)S(1)}, f32[1536,1,12]{0,1,2:T(1,128)}, u32[]{:S(2)}) copy-start(f32[1536,1,12]{0,1,2:T(1,128)} %param.39) | copy-start | bytes 221188
  153.5 39.2 %copy-start.13 = (f32[384,1,12]{0,1,2:T(1,128)S(1)}, f32[384,1,12]{0,1,2:T(1,128)}, u32[]{:S(2)}) copy-start(f32[384,1,12]{0,1,2:T(1,128)} %param.31) | copy-start | bytes 55300
  153.6 39.2 %copy-start.14 = (f32[384,3,1,12]{0,2,3,1:T(1,128)S(1)}, f32[384,3,1,12]{0,2,3,1:T(1,128)}, u32[]{:S(2)}) copy-start(f32[384,3,1,12]{0,2,3,1:T(1,128)} %param.29) | copy-start | bytes 165892
  153.6 39.2 %copy-start.19 = (f32[6,1,12]{2,1,0:T(1,128)S(1)}, f32[6,1,12]{2,1,0:T(1,128)}, u32[]{:S(2)}) copy-start(f32[6,1,12]{2,1,0:T(1,128)} %refs_6_.1) | copy-start | bytes 868
  192.8 0.8 copy-start.15
  193.6 0.7 copy-start.17
  194.3 0.7 copy-start.18
  195.0 0.7 copy-start.21
  195.7 0.7 copy-start.22
  196.4 0.7 copy-start.23
  197.1 0.7 copy-start.24
  197.7 0.7 copy-start.25
  198.4 0.7 copy-start.26
  199.1 0.7 copy-start.27
  199.7 0.7 copy-start.28
Sparse Core Ops, SparseCore 0:
  11.5 80.6 all-gather.6

commit v2 on v1

--- a/solution.py
+++ b/solution.py
@@ -108,12 +108,9 @@
     swap_ref,
     gathered_ref,
     result_ref,
-    part_ref,
-    small_s,
+    gin_ref,
     keep_out,
     send_out,
-    gqkv_out,
-    wqkv_out,
     load_sem,
     store_sem,
     x_ref,
@@ -124,7 +121,9 @@
     wout_s,
     wup_s,
     wdown_s,
-    buf_s,
+    small_s,
+    early_s,
+    late_s,
     bias_s,
     q_s,
     k_s,
@@ -214,8 +213,6 @@
     k_s[...] = keys
     kt_s[...] = keys.T
     values = (dot_nt(n1, wqkv_s[2]) + bqkv_ref[2:3, :]).astype(bf16)
-    store_wqkv = pltpu.make_async_copy(wqkv_s, wqkv_out, store_sem.at[2])
-    store_wqkv.start()
     v_s[...] = values
     vt_s[...] = values.T
 
@@ -291,6 +288,25 @@
     sums = jnp.sum(gh_s[:, row_units].astype(f32), axis=0, keepdims=True)
     for part in range(4):
         small_s[8 + part : 9 + part, :] = sums[:, HALF * part : HALF * part + HALF]
+
+    for g in range(8):
+        down = jnp.concatenate([stage_s[1, 8 * m + g] for m in range(4)], axis=0)
+        down = dot_nn(swap, down).astype(bf16)
+        for i in range(4):
+            to = 4 * g + i
+            slot = jnp.bitwise_xor(core, to % 2)
+            early_s[slot, to // 2, 0:48, :] = stage_s[0, to]
+            early_s[slot, to // 2, 48:96, :] = down[48 * i : 48 * i + 48]
+
+    def stores(source, rows, first):
+        return [
+            pltpu.make_async_copy(source.at[1 - i], target.at[:, rows, :], store_sem.at[first + i])
+            for i, target in enumerate((send_out, keep_out))
+        ]
+
+    store_early = stores(early_s, slice(0, 96), 0)
+    for copy in store_early:
+        copy.start()
 
     ga_s = gh_s.at[:, 0:D]
     gq_s = gh_s.at[:, D : 2 * D]
@@ -362,78 +378,41 @@
             ).astype(bf16)
 
     gq_s[...] = gqt_s[...].T
-    store_gqkv = pltpu.make_async_copy(gh_s.at[:, D : 4 * D], gqkv_out, store_sem.at[3])
-    store_gqkv.start()
 
     n1_half = n1_ref[:, col_half]
     row_rows = pl.ds(pl.multiple_of(row * HALF, HALF), HALF)
     put_attn(0, dot_nn(gqt_s[row_rows, :], n1_half))
     put_attn(1, dot_tn(gk_s[:, row_half], n1_half))
     put_attn(2, dot_tn(gv_s[:, row_half], n1_half))
-    small_s[0:2, :] = jnp.zeros((2, HALF), f32)
     small_s[6:7, :] = jnp.sum(gq_s[:, row_half].astype(f32), axis=0, keepdims=True)
     small_s[7:8, :] = jnp.sum(gv_s[:, row_half].astype(f32), axis=0, keepdims=True)
+    for tile in range(2):
+        ts = slice(256 * tile, 256 * tile + 256)
+        gn2_s[ts, :] = dot_nn(gh_s[ts, D : 4 * D], wqkv_s[...].reshape(3 * D, D))
+    gn1 = gn2_s[...]
+    unit1, inverse1 = moments(x_ref[...].astype(f32))
+    mid_s[...] += norm_back(gn1, unit1, inverse1, vec_ref[0:1, :])
+    gn2_s[0:2, :] = jnp.concatenate(
+        [jnp.sum(gn1 * unit1, axis=0, keepdims=True), jnp.sum(gn1, axis=0, keepdims=True)], axis=0
+    )
+    small_s[0:2, :] = gn2_s[0:2, col_half]
     small_s[12:16, :] = jnp.zeros((4, HALF), f32)
-    part_ref[...] = mid_s[row_tok, col_half] + og_ref[...]
-
+    gin_ref[...] = mid_s[row_tok, col_half] + og_ref[...]
+
+    put_small = small_s[...].astype(bf16)
     for g in range(8):
-        down = jnp.concatenate([stage_s[1, 8 * m + g] for m in range(4)], axis=0)
-        down = dot_nn(swap, down).astype(bf16)
         attn = jnp.concatenate([stage_s[2, 8 * j + g] for j in range(4)], axis=0)
         attn = dot_nn(swap, attn).astype(bf16)
         for i in range(4):
             to = 4 * g + i
             slot = jnp.bitwise_xor(core, to % 2)
-            part = slice(48 * i, 48 * i + 48)
-            buf_s[slot, to // 2, 0:48, :] = attn[part]
-            buf_s[slot, to // 2, 48:96, :] = stage_s[0, to]
-            buf_s[slot, to // 2, 96:144, :] = down[part]
-    store_send = pltpu.make_async_copy(buf_s.at[1], send_out, store_sem.at[0])
-    store_keep = pltpu.make_async_copy(buf_s.at[0], keep_out, store_sem.at[1])
-    store_send.start()
-    store_keep.start()
-    store_send.wait()
-    store_keep.wait()
-    store_wqkv.wait()
-    store_gqkv.wait()
-
-
-def input_kernel(
-    place_ref, x_ref, vec_ref, gqkv_ref, wqkv_ref, part_ref, some_ref, gin_ref, small_ref, gn1_s, back_s
-):
-    row_tok = pl.ds(pl.multiple_of(place_ref[0] * 256, 256), 256)
-    col_half = pl.ds(pl.multiple_of(place_ref[1] * HALF, 128), HALF)
-    for tile in range(2):
-        ts = slice(256 * tile, 256 * tile + 256)
-        gn1_s[ts, :] = dot_nn(gqkv_ref[ts, :], wqkv_ref[...].reshape(3 * D, D))
-    gn1 = gn1_s[...]
-    unit1, inverse1 = moments(x_ref[...].astype(f32))
-    back_s[...] = norm_back(gn1, unit1, inverse1, vec_ref[0:1, :])
-    gin_ref[...] = back_s[row_tok, col_half] + part_ref[...]
-    back_s[0:2, :] = jnp.concatenate(
-        [jnp.sum(gn1 * unit1, axis=0, keepdims=True), jnp.sum(gn1, axis=0, keepdims=True)], axis=0
-    )
-    small_ref[...] = some_ref[...]
-    small_ref[0:2, :] = back_s[0:2, col_half]
-
-
-def input_gradient(place, *operands):
-    whole = pl.BlockSpec(memory_space=VMEM)
-    return pl.pallas_call(
-        input_kernel,
-        in_specs=[pl.BlockSpec(memory_space=pltpu.SMEM)] + [whole] * len(operands),
-        out_specs=[whole] * 2,
-        out_shape=[
-            jax.ShapeDtypeStruct((256, HALF), f32),
-            jax.ShapeDtypeStruct((16, HALF), f32),
-        ],
-        scratch_shapes=[VMEM((TOK, D), f32), VMEM((TOK, D), f32)],
-        compiler_params=pltpu.CompilerParams(vmem_limit_bytes=32 * 1024 * 1024),
-        cost_estimate=pl.CostEstimate(
-            flops=6 * TOK * D * D, bytes_accessed=8 * 1024 * 1024, transcendentals=0
-        ),
-        name="input_gradient",
-    )(place, *operands)
+            late_s[slot, to // 2, 0:48, :] = attn[48 * i : 48 * i + 48]
+            late_s[slot, to // 2, 48:64, :] = put_small
+    store_late = stores(late_s, slice(96, 160), 2)
+    for copy in store_late:
+        copy.start()
+    for copy in store_early + store_late:
+        copy.wait()
 
 
 def layer(place, lengths, *operands):
@@ -445,15 +424,12 @@
         in_specs=[smem, smem, anywhere, whole, anywhere, anywhere]
         + [whole] * (len(operands) - 5)
         + [anywhere],
-        out_specs=[whole, whole, whole, anywhere, anywhere, anywhere, anywhere],
+        out_specs=[whole, whole, anywhere, anywhere],
         out_shape=[
             jax.ShapeDtypeStruct((256, HALF), f32),
             jax.ShapeDtypeStruct((256, HALF), f32),
-            jax.ShapeDtypeStruct((16, HALF), f32),
-            jax.ShapeDtypeStruct((16, 144, HALF), bf16),
-            jax.ShapeDtypeStruct((16, 144, HALF), bf16),
-            jax.ShapeDtypeStruct((TOK, 3 * D), bf16),
-            jax.ShapeDtypeStruct((3, D, D), bf16),
+            jax.ShapeDtypeStruct((16, 160, HALF), bf16),
+            jax.ShapeDtypeStruct((16, 160, HALF), bf16),
         ],
         scratch_shapes=[
             pltpu.SemaphoreType.DMA((15,)),
@@ -466,7 +442,9 @@
             VMEM((D, D), bf16),
             VMEM((64, 48, D), bf16),
             VMEM((D, FF), bf16),
-            VMEM((2, 16, 144, HALF), bf16),
+            VMEM((16, HALF), f32),
+            VMEM((2, 16, 96, HALF), bf16),
+            VMEM((2, 16, 64, HALF), bf16),
             VMEM((TOK, TOK), f32),
             VMEM((TOK, D), bf16),
             VMEM((TOK, D), bf16),
@@ -490,22 +468,21 @@
 
 
 def adam_kernel(data_ref, *refs):
-    parts_ref, smalls_ref = refs[0:2]
-    masters, firsts, seconds = refs[2:9], refs[9:16], refs[16:23]
-    grads, news, updates = refs[23:30], refs[30:37], refs[37:44]
+    parts_ref = refs[0]
+    masters, firsts, seconds = refs[1:8], refs[8:15], refs[15:22]
+    grads, news, updates = refs[22:29], refs[29:36], refs[36:43]
     total = parts_ref[0].astype(f32)
     for i in range(1, 16):
         total = total + parts_ref[i].astype(f32)
     data = data_ref[0]
-    lows = jnp.sum(smalls_ref[...], axis=0)
-    small = pltpu.roll(lows[0:8], HALF - data * 12, 1)
-    wide = jnp.concatenate([lows[8 + m : 9 + m] for m in range(4)], axis=1)
+    small = pltpu.roll(total[144:152], HALF - data * 12, 1)
+    wide = jnp.concatenate([total[152 + m : 153 + m] for m in range(4)], axis=1)
     wide = pltpu.roll(jnp.broadcast_to(wide, (8, FF // 2)), FF // 2 - data * 48, 1)
     gradients = (
-        total[0:36].reshape(36, 1, HALF),
-        total[36:48].reshape(12, 1, HALF),
-        total[48:96],
-        jnp.concatenate([total[96 + 12 * m : 108 + 12 * m] for m in range(4)], axis=1).reshape(
+        total[96:132].reshape(36, 1, HALF),
+        total[132:144].reshape(12, 1, HALF),
+        total[0:48],
+        jnp.concatenate([total[48 + 12 * m : 60 + 12 * m] for m in range(4)], axis=1).reshape(
             12, 1, 4 * HALF
         ),
         small[0:6, 0:12].reshape(6, 1, 12),
@@ -521,17 +498,17 @@
         updates[i][...] = updated
 
 
-def update_masters(data, parts, smalls, masters, firsts, seconds):
+def update_masters(data, parts, masters, firsts, seconds):
     whole = pl.BlockSpec(memory_space=VMEM)
     shapes = [jax.ShapeDtypeStruct(m.shape, f32) for m in masters]
     results = pl.pallas_call(
         adam_kernel,
-        in_specs=[pl.BlockSpec(memory_space=pltpu.SMEM)] + [whole] * 23,
+        in_specs=[pl.BlockSpec(memory_space=pltpu.SMEM)] + [whole] * 22,
         out_specs=[whole] * 21,
         out_shape=shapes * 3,
         compiler_params=pltpu.CompilerParams(vmem_limit_bytes=32 * 1024 * 1024),
         name="update_masters",
-    )(data, parts, smalls, *masters, *firsts, *seconds)
+    )(data, parts, *masters, *firsts, *seconds)
     return results[0:7], results[7:14], results[14:21]
 
 
@@ -626,9 +603,8 @@
     normed_one = (unit_one * vec[0:1] + vec[1:2]).astype(bf16)
 
     place = jnp.stack([lax.axis_index("row"), lax.axis_index("col"), lax.axis_index("core")])
-    place = place.astype(jnp.int32)
-    result, part, some, keep, send, gqkv, wqkv = layer(
-        place,
+    result, grad_in, keep, send = layer(
+        place.astype(jnp.int32),
         seq_lengths,
         rows_full,
         normed_one,
@@ -643,12 +619,9 @@
 
     other = lax.ppermute(send, "core", [(0, 1), (1, 0)])
     both = (keep.astype(f32) + other.astype(f32)).astype(bf16)
-    both, part = lax.optimization_barrier((both, part))
     parts = lax.all_to_all(both, ("y", "x"), 0, 0, tiled=True)
-    grad_in, small = input_gradient(place, rows_full, vec, gqkv, wqkv, part, some)
-    smalls = lax.all_gather(small, DP, axis=0, tiled=False)
     data = lax.axis_index(DP).astype(jnp.int32).reshape(1)
-    grads, news, updates = update_masters(data, parts, smalls, masters, firsts, seconds)
+    grads, news, updates = update_masters(data, parts, masters, firsts, seconds)
     outputs = [result, grad_in]
     for triple in zip(unflat(*grads), unflat(*news), unflat(*updates)):
         outputs += triple

time: 212 us -> 193 us (0.910)
  blocking collectives: 90.3 us -> 55.1 us
  waiting for transfers between devices: 18.9 us -> 49.9 us
  local copies, waits for them, and re-layouts: 18.9 us -> 6.23 us
    all_gather x1 -> x0, blocking collectives: 35.2 us -> none  [on_device(): smalls = lax.all_gather(small, DP, axis=0, tiled=False)]
    all_to_all x1, waiting for transfers between devices: 0.01 us -> 30.6 us  [on_device(): parts = lax.all_to_all(both, ('y', 'x'), 0, 0, tiled=True)]
    unnamed x64 -> x50, local copies, waits for them, and re-layouts: 14 us -> 1.26 us
    pallas_call x1 -> x0, Pallas kernels: 3.89 us -> none  [input_gradient(): pl.pallas_call(input_kernel, in_specs=[pl.BlockSpec(memory_space=pltpu.SM...]
  transfers between devices with their start and end apart: 3 -> 3, of which waited for: 2 -> 3; matrix products, arithmetic and copies ran while one was open for 6% -> 7% of each run, Pallas kernels for 2% -> 0%
where the time goes in v2:
time: 193 us; the launch traced here: 190 us
  blocking collectives  55.1 us (29%)
  waiting for transfers between devices  49.9 us (26%)
  Pallas kernels  47.2 us (24%)
  between operations  14.7 us (8%)
  other arithmetic  9.89 us (5%)
  starting transfers between devices  7.05 us (4%)
  local copies, waits for them, and re-layouts  6.23 us (3%)
    pallas_call x1, Pallas kernels, layer(): pl.pallas_call(layer_kernel, in_specs=[smem, smem, anywhere, whole, anywh...  44.1 us
    all_to_all x1, waiting for transfers between devices, on_device(): parts = lax.all_to_all(both, ('y', 'x'), 0, 0, tiled=True)  30.6 us
    all_gather x1, blocking collectives, on_device(): smalls = lax.all_gather(four[:, 256, 0:144], DP, axis=0, tiled=False)  26.8 us
    all_gather x1, waiting for transfers between devices, on_device(): lax.all_gather(pack_masters(*masters[:4]), ALL, axis=0, tiled=False)  15.4 us
    all_gather x1, blocking collectives, on_device(): lax.all_gather(jnp.concatenate([block_in, small], axis=0), ('row', 'col')...  14.6 us
    all_gather x1, blocking collectives, on_device(): lax.all_gather(out_grad.astype(bf16), ('row', 'col'), axis=0, tiled=False)  13.8 us
    all_to_all x1, starting transfers between devices, on_device(): parts = lax.all_to_all(both, ('y', 'x'), 0, 0, tiled=True)  6.69 us
    ppermute x1, waiting for transfers between devices, on_device(): other = lax.ppermute(send, 'core', [(0, 1), (1, 0)])  3.94 us
  transfers between devices with their start and end apart: 3, of which 3 were waited for; matrix products, arithmetic and copies ran while one was open for 7% of the time, Pallas kernels for 0%

profile of v2, /device:TPU:1, one launch (start us, length us, event | category | flops | bytes accessed | tf_op | source)
XLA Modules:
  0.0 190.1 jit_solution(4781947474651379593)
XLA Ops:
  7.2 1.7 pack_masters.1
  8.9 0.7 convert_reduce_fusion.3
  9.6 0.1 concatenate.22
  9.7 0.7 convert.16
  10.4 0.7 convert_reduce_fusion.2
  11.1 0.1 concatenate.21
  11.2 0.1 pad.9.clone
  11.2 1.0 maximum_maximum_fusion
  12.3 14.6 %all-gather = bf16[1088,384]{1,0:T(8,128)(2,1)S(1)} all-gather(bf16[272,384]{1,0:T(8,128)(2,1)S(1)} %maximum_maximum_fusion), channel_id=2, replica_groups=mesh['y'=4,'x'=4,'core'=2,'row'=2,'col'=2] {'row','col'}, dimensions={0}, use_global_device_ids=true | all-gather | bytes 1044480 | tf_op jit(solution)/shard_map/all_gather | solution.py:584
  26.9 0.1 slice.46
  27.0 26.8 %all-gather.1 = bf16[128,1,144]{2,1,0:T(2,128)(2,1)S(1)} all-gather(bf16[4,1,144]{2,1,0:T(2,128)(2,1)S(1)} %slice.47), channel_id=3, replica_groups=mesh['y'=4,'x'=4,'core'=2,'row'=2,'col'=2] {'y','x','core'}, dimensions={0}, use_global_device_ids=true | all-gather | bytes 38016 | tf_op jit(solution)/shard_map/all_gather | solution.py:592
  53.7 0.4 convert_reduce_fusion.1
  54.1 0.1 reshape.223
  54.2 0.1 slice.54
  54.3 0.1 slice.51
  54.5 13.8 %all-gather.2 = bf16[1024,384]{1,0:T(8,128)(2,1)S(1)} all-gather(bf16[256,384]{1,0:T(8,128)(2,1)S(1)} %convert_element_type.41), channel_id=4, replica_groups=mesh['y'=4,'x'=4,'core'=2,'row'=2,'col'=2] {'row','col'}, dimensions={0}, use_global_device_ids=true | all-gather | bytes 983040 | tf_op jit(solution)/shard_map/all_gather | solution.py:600
  68.3 0.8 copy.65
  69.1 1.0 copy.75
  70.1 0.8 copy.61
  70.9 0.2 convert_reduce_fusion
  71.1 0.1 copy.72
  71.3 0.4 fusion.1
  71.7 0.7 reshape.208.bup_ref
  72.4 0.1 copy.67
  72.4 0.1 copy.68
  72.5 0.1 slice.42
  72.7 0.1 copy.69
  72.8 0.1 slice.44
  72.9 0.1 copy.62
  73.0 0.1 copy.66
  73.1 0.1 copy.63
  73.2 0.1 mul.55
  73.3 0.1 copy.64
  73.4 0.1 add.35
  73.5 0.1 reshape.207
  73.7 0.6 concatenate.25.vec_ref
  74.3 0.1 pad.2.clone
  74.4 0.6 pad_add_fusion.place_ref
  74.9 0.7 pad_maximum_fusion.bqkv_ref
  75.6 1.3 add_convert_fusion.1.n1_ref
  76.9 15.4 %all-gather.6.cloned.1.call-done = bf16[18432,384]{1,0:T(8,128)(2,1)} async-done(((bf16[144,384]{1,0:T(8,128)(2,1)}), bf16[18432,384]{1,0:T(8,128)(2,1)}) %all-gather.6.cloned.1.call-update) | async-done | bytes 14155792 | tf_op jit(solution)/shard_map/all_gather | solution.py:577
  92.2 44.1 %layer.1 = (f32[256,384]{1,0:T(8,128)}, f32[256,384]{1,0:T(8,128)}, bf16[16,160,384]{2,1,0:T(8,128)(2,1)}, bf16[16,160,384]{2,1,0:T(8,128)(2,1)}) custom-call(s32[3]{0:T(128)} %pad_add_fusion.place_ref, s32[1,4]{1,0:T(1,128)} %lengths_ref.1, bf16[512,768]{1,0:T(8,128)(2,1)} %bitcast.112, bf16[512,768]{1,0:T(8,128)(2,1)} %add_convert_fusion.1.n1_ref, ...), custom_call_target="tpu_custom_call" | custom-call | tf_op jit(solution)/shard_map/layer/pallas_call | solution.py:422
  136.3 0.3 collective-permute-start
  136.6 3.9 %collective-permute-done = bf16[16,160,384]{2,1,0:T(8,128)(2,1)S(1)} collective-permute-done((bf16[16,160,384]{2,1,0:T(8,128)(2,1)}, bf16[16,160,384]{2,1,0:T(8,128)(2,1)S(1)}, u32[]{:S(2)}, u32[]{:S(2)}) %collective-permute-start) | collective-permute-done | bytes 1966112 | tf_op jit(solution)/shard_map/ppermute | solution.py:620
  140.6 3.3 %add_convert_fusion = bf16[16,160,384]{2,1,0:T(8,128)(2,1)} fusion(bf16[16,160,384]{2,1,0:T(8,128)(2,1)S(1)} %collective-permute-done, bf16[16,160,384]{2,1,0:T(8,128)(2,1)} %get-tuple-element.50), kind=kLoop, calls=%fused_computation | loop fusion | flops 3932160 | bytes 5898240 | tf_op jit(solution)/shard_map/convert_element_type | solution.py:621
  144.1 6.7 %all-to-all-start = ((bf16[16,160,384]{2,1,0:T(8,128)(2,1)}), bf16[16,160,384]{2,1,0:T(8,128)(2,1)S(1)}, u32[]{:S(2)}, u32[]{:S(2)}) async-start(bf16[16,160,384]{2,1,0:T(8,128)(2,1)} %add_convert_fusion), calls=%async_computation | async-start | bytes 3932160 | tf_op jit(solution)/shard_map/all_to_all | solution.py:622
  150.8 30.6 %all-to-all-done.refs_0_ = bf16[16,160,384]{2,1,0:T(8,128)(2,1)S(1)} async-done(((bf16[16,160,384]{2,1,0:T(8,128)(2,1)}), bf16[16,160,384]{2,1,0:T(8,128)(2,1)S(1)}, u32[]{:S(2)}, u32[]{:S(2)}) %all-to-all-start) | async-done | bytes 1966112 | tf_op jit(solution)/shard_map/all_to_all | solution.py:622
  181.6 1.5 update_masters.1
  (60 shorter events, 0.3 us)
Async XLA Ops:
  7.2 85.1 %all-gather.6.cloned.1.call-start = ((), (), s32[]{:S(2)}) async-start(), calls=%async_computation.1 | async-start | bytes 14266368 | tf_op jit(solution)/shard_map/all_gather | solution.py:577
  12.3 42.2 %copy-start.22 = (f32[256,384]{1,0:T(8,128)S(1)}, f32[256,384]{1,0:T(8,128)}, u32[]{:S(2)}) copy-start(f32[256,384]{1,0:T(8,128)} %og_hbm.1) | copy-start | bytes 1179652
  71.3 5.6 %copy-start.21 = (bf16[64,8,2,384]{3,1,2,0:T(8,128)(2,1)}, bf16[64,8,2,384]{3,1,2,0:T(8,128)(2,1)S(1)}, u32[]{:S(2)}) copy-start(bf16[64,8,2,384]{3,1,2,0:T(8,128)(2,1)S(1)} %copy.72) | copy-start | bytes 2359300
  136.3 4.3 %collective-permute-start = (bf16[16,160,384]{2,1,0:T(8,128)(2,1)}, bf16[16,160,384]{2,1,0:T(8,128)(2,1)S(1)}, u32[]{:S(2)}, u32[]{:S(2)}) collective-permute-start(bf16[16,160,384]{2,1,0:T(8,128)(2,1)} %get-tuple-element.51), channel_id=1, source_target_pairs={{0,4},{4,0},{1,5},{5,1},{2,6},{6,2},{3,7},{7,3},{8,12},{12,8},{9,1... | collective-permute-start | bytes 5898248 | tf_op jit(solution)/shard_map/ppermute | solution.py:620
  143.9 37.5 %copy-start = (f32[384,1,48]{0,2,1:T(8,128)S(1)}, f32[384,1,48]{0,2,1:T(8,128)}, u32[]{:S(2)}) copy-start(f32[384,1,48]{0,2,1:T(8,128)} %param.34) | copy-start | bytes 221188
  143.9 37.5 %copy-start.1 = (f32[1536,1,12]{0,1,2:T(1,128)S(1)}, f32[1536,1,12]{0,1,2:T(1,128)}, u32[]{:S(2)}) copy-start(f32[1536,1,12]{0,1,2:T(1,128)} %param.37) | copy-start | bytes 221188
  143.9 37.5 %copy-start.2 = (f32[384,3,1,12]{0,2,3,1:T(1,128)S(1)}, f32[384,3,1,12]{0,2,3,1:T(1,128)}, u32[]{:S(2)}) copy-start(f32[384,3,1,12]{0,2,3,1:T(1,128)} %param.28) | copy-start | bytes 165892
  143.9 37.5 %copy-start.3 = (f32[384,1,48]{0,2,1:T(8,128)S(1)}, f32[384,1,48]{0,2,1:T(8,128)}, u32[]{:S(2)}) copy-start(f32[384,1,48]{0,2,1:T(8,128)} %param.35) | copy-start | bytes 221188
  143.9 37.5 %copy-start.4 = (f32[1536,1,12]{0,1,2:T(1,128)S(1)}, f32[1536,1,12]{0,1,2:T(1,128)}, u32[]{:S(2)}) copy-start(f32[1536,1,12]{0,1,2:T(1,128)} %param.38) | copy-start | bytes 221188
  143.9 37.5 %copy-start.5 = (f32[384,1,48]{0,2,1:T(8,128)S(1)}, f32[384,1,48]{0,2,1:T(8,128)}, u32[]{:S(2)}) copy-start(f32[384,1,48]{0,2,1:T(8,128)} %param.36) | copy-start | bytes 221188
  143.9 37.5 %copy-start.6 = (f32[1536,1,12]{0,1,2:T(1,128)S(1)}, f32[1536,1,12]{0,1,2:T(1,128)}, u32[]{:S(2)}) copy-start(f32[1536,1,12]{0,1,2:T(1,128)} %param.39) | copy-start | bytes 221188
  144.0 37.5 %copy-start.7 = (f32[384,1,12]{0,1,2:T(1,128)S(1)}, f32[384,1,12]{0,1,2:T(1,128)}, u32[]{:S(2)}) copy-start(f32[384,1,12]{0,1,2:T(1,128)} %param.31) | copy-start | bytes 55300
  144.0 37.5 %copy-start.8 = (f32[384,3,1,12]{0,2,3,1:T(1,128)S(1)}, f32[384,3,1,12]{0,2,3,1:T(1,128)}, u32[]{:S(2)}) copy-start(f32[384,3,1,12]{0,2,3,1:T(1,128)} %param.29) | copy-start | bytes 165892
  144.0 37.5 %copy-start.9 = (f32[384,3,1,12]{0,2,3,1:T(1,128)S(1)}, f32[384,3,1,12]{0,2,3,1:T(1,128)}, u32[]{:S(2)}) copy-start(f32[384,3,1,12]{0,2,3,1:T(1,128)} %param.30) | copy-start | bytes 165892
  144.0 37.5 %copy-start.10 = (f32[384,1,12]{0,1,2:T(1,128)S(1)}, f32[384,1,12]{0,1,2:T(1,128)}, u32[]{:S(2)}) copy-start(f32[384,1,12]{0,1,2:T(1,128)} %param.32) | copy-start | bytes 55300
  144.0 37.5 %copy-start.11 = (f32[384,1,12]{0,1,2:T(1,128)S(1)}, f32[384,1,12]{0,1,2:T(1,128)}, u32[]{:S(2)}) copy-start(f32[384,1,12]{0,1,2:T(1,128)} %param.33) | copy-start | bytes 55300
  144.0 37.5 %copy-start.12 = (f32[6,1,12]{2,1,0:T(1,128)S(1)}, f32[6,1,12]{2,1,0:T(1,128)}, u32[]{:S(2)}) copy-start(f32[6,1,12]{2,1,0:T(1,128)} %refs_5_.1) | copy-start | bytes 868
  144.0 37.5 %copy-start.13 = (f32[6,1,12]{2,1,0:T(1,128)S(1)}, f32[6,1,12]{2,1,0:T(1,128)}, u32[]{:S(2)}) copy-start(f32[6,1,12]{2,1,0:T(1,128)} %refs_12_.1) | copy-start | bytes 868
  144.0 37.5 %copy-start.14 = (f32[6,1,12]{2,1,0:T(1,128)S(1)}, f32[6,1,12]{2,1,0:T(1,128)}, u32[]{:S(2)}) copy-start(f32[6,1,12]{2,1,0:T(1,128)} %refs_19_.1) | copy-start | bytes 868
  144.1 37.5 %copy-start.15 = (f32[2,1,12]{2,1,0:T(1,128)S(1)}, f32[2,1,12]{2,1,0:T(1,128)}, u32[]{:S(2)}) copy-start(f32[2,1,12]{2,1,0:T(1,128)} %refs_6_.1) | copy-start | bytes 292
  144.1 37.5 %copy-start.16 = (f32[2,1,12]{2,1,0:T(1,128)S(1)}, f32[2,1,12]{2,1,0:T(1,128)}, u32[]{:S(2)}) copy-start(f32[2,1,12]{2,1,0:T(1,128)} %refs_13_.1) | copy-start | bytes 292
  144.1 37.5 %copy-start.17 = (f32[2,1,12]{2,1,0:T(1,128)S(1)}, f32[2,1,12]{2,1,0:T(1,128)}, u32[]{:S(2)}) copy-start(f32[2,1,12]{2,1,0:T(1,128)} %refs_20_.1) | copy-start | bytes 292
  144.1 37.5 %copy-start.18 = (f32[1,48]{1,0:T(1,128)S(1)}, f32[1,48]{1,0:T(1,128)}, u32[]{:S(2)}) copy-start(f32[1,48]{1,0:T(1,128)} %refs_7_.1) | copy-start | bytes 580
  144.1 37.5 %copy-start.19 = (f32[1,48]{1,0:T(1,128)S(1)}, f32[1,48]{1,0:T(1,128)}, u32[]{:S(2)}) copy-start(f32[1,48]{1,0:T(1,128)} %refs_14_.1) | copy-start | bytes 580
  144.1 37.5 %copy-start.20 = (f32[1,48]{1,0:T(1,128)S(1)}, f32[1,48]{1,0:T(1,128)}, u32[]{:S(2)}) copy-start(f32[1,48]{1,0:T(1,128)} %refs_21_.1) | copy-start | bytes 580
  144.1 37.3 %all-to-all-start = ((bf16[16,160,384]{2,1,0:T(8,128)(2,1)}), bf16[16,160,384]{2,1,0:T(8,128)(2,1)S(1)}, u32[]{:S(2)}, u32[]{:S(2)}) async-start(bf16[16,160,384]{2,1,0:T(8,128)(2,1)} %add_convert_fusion), calls=%async_computation | async-start | bytes 3932160 | tf_op jit(solution)/shard_map/all_to_all | solution.py:622
Sparse Core Ops, SparseCore 0:
  11.5 80.6 all-gather.5
